TPU v7x, 256 devices: a whole 4x4x8 slice. The times are simulated.
256 devices in a mesh: vec: 32 (over y, x, core), row: 8 (over z).
Axes of the slice: x: 4, y: 4, z: 8, core: 2. Of those that a mesh axis runs over, the one named last changes fastest.
Arguments:
- blocks: bfloat16 [8192, 1024, 128], P('vec', 'row'), may hold values from -6 to 6
- block_vector: int32 [8, 8192], P('row', 'vec'), may hold values from 0 to 127, as said below
- block_pair: int32 [8, 8192], P('row', 'vec'), may hold values from 0 to 71
- block_count: int32 [8, 32], P('row', 'vec'), may hold values from 8 to 256, as said below
- occ_order: int32 [288], replicated, may hold values from 0 to 287, each once
- occ_coeffs: bfloat16 [3072, 288], P('row'), may hold values from -0.109375 to 0.109375
- vir_coeffs: bfloat16 [3072, 2688], P('row'), may hold values from -0.109375 to 0.109375
Outputs:
- ov_blocks: bfloat16 [2688, 288, 128], P('row', 'vec')
- oo_blocks: bfloat16 [288, 288, 128], P('row', 'vec')
Inputs may be any that keep to these rules, and one draw needn't show every extreme that they name: `block_vector`: of one device's valid slots, at most 8 name vectors of one owner (vector // 4); in each row index one owner receives exactly 8 valid slots from every device. `block_count`: in each row index some device has all 256 slots valid.
All inputs are finite; a program needn't handle non-finite values.
Results may differ from a plain program's by a relative error of at most 0.0052.
Values may be sent and summed in bfloat16 or wider, within the bound.
A program may use at most 128 MiB of HBM per device.

v0:
```python
import jax
import jax.numpy as jnp
from jax import lax
from jax.sharding import PartitionSpec as P

NAO = 3072
VEC_DEV = 4


def on_device(blocks, block_vector, block_pair, block_count, occ_order, occ_coeffs, vir_coeffs):
    owners = lax.axis_size("vec")
    slot_total = blocks.shape[0]
    capacity = slot_total // owners
    tile_size = blocks.shape[2]
    row_span = vir_coeffs.shape[0]
    tile_rows = row_span // tile_size
    tiles_across = NAO // tile_size
    pair_total = tile_rows * tiles_across
    dropped = VEC_DEV * pair_total
    slot_index = jnp.arange(slot_total, dtype=jnp.int32)
    is_valid = slot_index < block_count[0, 0]
    vectors = block_vector[0]
    owner_index = vectors // VEC_DEV
    chosen = (owner_index[:, None] == jnp.arange(owners, dtype=jnp.int32)[None, :]).astype(
        jnp.int32
    )
    member = chosen * is_valid[:, None].astype(jnp.int32)
    owner_rank = jnp.sum((jnp.cumsum(member, axis=0) - member) * chosen, axis=1)
    position = jnp.where(is_valid, owner_index * capacity + owner_rank, slot_total)
    source = jnp.zeros((slot_total,), jnp.int32).at[position].set(slot_index, mode="drop")
    filled = jnp.zeros((slot_total,), jnp.bool_).at[position].set(True, mode="drop")
    slot_code = vectors % VEC_DEV * pair_total + block_pair[0]
    send_code = jnp.where(filled, slot_code[source], dropped).reshape(owners, capacity)
    send_tiles = blocks[source].reshape(owners, capacity, tile_size, tile_size)
    recv_tiles, recv_code = (
        lax.all_to_all(send_tiles, "vec", split_axis=0, concat_axis=0, tiled=True),
        lax.all_to_all(send_code, "vec", split_axis=0, concat_axis=0, tiled=True),
    )
    placed = (
        jnp.zeros((dropped, tile_size, tile_size), jnp.float32)
        .at[recv_code.reshape(-1)]
        .add(recv_tiles.reshape(-1, tile_size, tile_size).astype(jnp.float32), mode="drop")
    )
    matrix = placed.reshape(VEC_DEV, tile_rows, tiles_across, tile_size, tile_size)
    matrix = matrix.transpose(0, 1, 3, 2, 4).reshape(VEC_DEV, row_span, NAO).astype(jnp.bfloat16)
    perm_local = occ_coeffs[:, occ_order]
    occ_full = lax.all_gather(perm_local, "row", axis=0, tiled=True)
    half_moved = jnp.einsum(
        "vrm,mi->vri", matrix, occ_full, preferred_element_type=jnp.float32
    ).astype(jnp.bfloat16)
    ov_part = jnp.einsum("ma,vmi->aiv", vir_coeffs, half_moved, preferred_element_type=jnp.float32)
    oo_part = jnp.einsum("mj,vmi->jiv", perm_local, half_moved, preferred_element_type=jnp.float32)
    ov_sum, oo_sum = (
        lax.psum_scatter(ov_part, "row", scatter_dimension=0, tiled=True),
        lax.psum_scatter(oo_part, "row", scatter_dimension=0, tiled=True),
    )
    ov_out, oo_out = (
        lax.all_to_all(ov_sum.astype(jnp.bfloat16), "vec", split_axis=1, concat_axis=2, tiled=True),
        lax.all_to_all(oo_sum.astype(jnp.bfloat16), "vec", split_axis=1, concat_axis=2, tiled=True),
    )
    return (ov_out, oo_out)


def solution(mesh):
    placed = (
        P("vec", "row", None),
        P("row", "vec"),
        P("row", "vec"),
        P("row", "vec"),
        P(),
        P("row", None),
        P("row", None),
    )
    return jax.shard_map(
        on_device,
        mesh=mesh,
        in_specs=placed,
        out_specs=(P("row", "vec", None), P("row", "vec", None)),
        check_vma=False,
    )
```

profile of v0, /device:TPU:56, one launch (start us, length us, event | category | flops | bytes accessed | tf_op | source)
XLA Modules:
  0.0 511.0 jit_solution(7865104045573456654)
XLA Ops:
  7.2 0.0 copy-start
  8.0 0.7 and_select_fusion.2
  8.7 0.6 reduce-window.6
  9.3 0.2 slice_reduce_fusion
  9.5 0.7 fusion.12
  10.2 0.1 fusion.9
  10.3 0.7 compare_select_fusion.1
  11.0 1.4 scatter_custom_fusion.1
  12.5 1.9 gather_fusion
  14.4 1.5 scatter_custom_fusion
  15.9 0.7 all_to_all.35
  16.6 7.4 %all-to-all-start = ((s32[32,1,8]{2,1,0:T(1,128)}), s32[32,1,8]{2,1,0:T(1,128)S(1)}, u32[]{:S(2)}, u32[]{:S(2)}) async-start(s32[32,1,8]{2,1,0:T(1,128)} %bitcast.8), calls=%async_computation | async-start | bytes 32768 | tf_op jit(solution)/shard_map/all_to_all | solution.py:37
  24.0 11.8 %gather_fusion.1 = bf16[256,128,128]{2,1,0:T(8,128)(2,1)} fusion(bf16[256,128,128]{2,1,0:T(8,128)(2,1)} %param.7, s32[1024]{0:T(1024)S(1)} %pad_clamp_fusion.1), kind=kCustom, calls=%fused_computation.1 | custom fusion | bytes 16778240 | tf_op jit(solution)/shard_map/gather | solution.py:34
  35.8 0.0 all-to-all-done
  35.8 0.0 copy-start.3
  35.8 0.0 copy-start.1
  35.8 7.8 %all-to-all-start.1 = ((bf16[32,8,128,128]{3,2,1,0:T(8,128)(2,1)}), bf16[32,8,128,128]{3,2,1,0:T(8,128)(2,1)}, u32[]{:S(2)}, u32[]{:S(2)}) async-start(bf16[32,8,128,128]{3,2,1,0:T(8,128)(2,1)} %bitcast.85), calls=%async_computation.1 | async-start | bytes 16777216 | tf_op jit(solution)/shard_map/all_to_all | solution.py:36
  43.6 0.0 all-gather.3.cloned.1.call-start
  43.6 0.0 copy-done.3
  43.7 0.0 copy-done.1
  43.7 2.5 gather_fusion.2
  46.2 0.0 all-gather.3.cloned.1.call-update
  46.2 0.0 reduce-scatter.4.cloned.1.call-start
  46.2 0.5 broadcast.213
  46.8 0.7 reduce.5
  47.5 0.1 reshape.190
  47.6 97.2 %all-to-all-done.1 = bf16[32,8,128,128]{3,2,1,0:T(8,128)(2,1)} async-done(((bf16[32,8,128,128]{3,2,1,0:T(8,128)(2,1)}), bf16[32,8,128,128]{3,2,1,0:T(8,128)(2,1)}, u32[]{:S(2)}, u32[]{:S(2)}) %all-to-all-start.1) | async-done | bytes 8388640 | tf_op jit(solution)/shard_map/all_to_all | solution.py:36
  144.7 11.3 %bitcast_convert_fusion = f32[256,128,128]{2,1,0:T(8,128)} fusion(bf16[32,8,128,128]{3,2,1,0:T(8,128)(2,1)} %all-to-all-done.1), kind=kLoop, calls=%fused_computation.6 | loop fusion | flops 4194304 | bytes 25165824 | tf_op jit(solution)/shard_map/convert_element_type | solution.py:42
  156.0 8.9 %broadcast_in_dim.33 = f32[288,128,128]{2,1,0:T(8,128)} broadcast(f32[]{:T(128)} %constant.41.clone.1), dimensions={} | broadcast | bytes 18874372 | tf_op jit(solution)/shard_map/broadcast_in_dim | solution.py:40
  164.9 51.9 %scatter_fusion = f32[288,128,128]{2,1,0:T(8,128)} fusion(f32[288,128,128]{2,1,0:T(8,128)} %broadcast_in_dim.33, s32[256]{0:T(256)S(1)} %bitcast.94, f32[256,128,128]{2,1,0:T(8,128)} %bitcast_convert_fusion), kind=kCustom, calls=%fused_computation.5 | custom fusion | flops 4194304 | bytes 50332672 | tf_op jit(solution)/shard_map/scatter-add | solution.py:42
  216.7 11.5 %convert_element_type.43 = bf16[288,128,128]{2,1,0:T(8,128)(2,1)} convert(f32[288,128,128]{2,1,0:T(8,128)} %scatter_fusion) | non-fusion elementwise | flops 4718592 | bytes 28311552 | tf_op jit(solution)/shard_map/convert_element_type | solution.py:45
  228.3 14.7 %copy.28 = bf16[4,3,128,24,128]{4,3,2,1,0:T(8,128)(2,1)} copy(bf16[4,3,128,24,128]{4,2,3,1,0:T(8,128)(2,1)} %bitcast.84) | data formatting | bytes 18874368 | tf_op jit(solution)/shard_map/convert_element_type | solution.py:45
  242.9 14.8 %convert_element_type.46 = bf16[4,384,3072]{2,1,0:T(8,128)(2,1)} reshape(bf16[4,3,128,24,128]{4,3,2,1,0:T(8,128)(2,1)} %copy.28) | data formatting | bytes 18874368 | tf_op jit(solution)/shard_map/convert_element_type | solution.py:45
  257.8 0.0 all-gather.3.cloned.1.call-done
  257.8 7.1 %fusion.3 = bf16[4,384,288]{1,2,0:T(8,128)(2,1)S(1)} fusion(bf16[4,384,3072]{2,1,0:T(8,128)(2,1)} %convert_element_type.46, bf16[3072,288]{0,1:T(8,128)(2,1)} %all-gather.3.cloned.1.call-done), kind=kOutput, calls=%fused_computation.12 | convolution fusion | flops 2718351360 | bytes 12091392 | tf_op jit(solution)/shard_map/vrm,mi->vri/dot_general | solution.py:48
  264.9 0.0 copy-done
  264.9 6.5 %convolution_bitcast_fusion = f32[2688,288,4]{0,1,2:T(8,128)} fusion(bf16[4,384,288]{1,2,0:T(8,128)(2,1)S(1)} %fusion.3, bf16[384,2688]{1,0:T(8,128)(2,1)S(1)} %copy-done), kind=kOutput, calls=%fused_computation.7 | convolution fusion | flops 2378170368 | bytes 15335424 | tf_op jit(solution)/shard_map/ma,vmi->aiv/dot_general | solution.py:51
  271.4 17.2 %copy.36 = f32[2688,288,4]{1,2,0:T(4,128)} copy(f32[2688,288,4]{0,1,2:T(8,128)} %convolution_bitcast_fusion) | data formatting | bytes 24772608
  288.6 17.6 %reshape.248 = f32[2688,1152]{1,0:T(8,128)} reshape(f32[2688,4,288]{2,1,0:T(4,128)} %bitcast.83) | data formatting | bytes 24772608
  306.2 0.0 copy-start.4
  306.2 0.0 copy-start.2
  306.2 0.0 reduce-scatter.4.cloned.1.call-update
  306.2 0.6 copy-done.4
  306.9 0.6 dynamic-slice
  308.1 0.0 copy-done.2
  308.1 1.9 convolution_bitcast_fusion.1
  310.0 3.7 copy.31
  313.7 90.8 %all-reduce.2 = bf16[288,288,4]{1,2,0:T(4,128)(2,1)S(1)} all-reduce(f32[288,288,4]{1,2,0:T(4,128)} %copy.31), channel_id=4, replica_groups=mesh['vec'=32,'row'=8] {'row'}, use_global_device_ids=true, to_apply=%region_7.8.clone | all-reduce | flops 331776 | bytes 1990656
  404.5 0.3 copy.32
  404.8 1.0 reshape.265
  405.8 9.0 %all-to-all-start.3 = ((bf16[32,2,648]{2,1,0:T(2,128)(2,1)}), bf16[32,2,648]{2,1,0:T(2,128)(2,1)S(1)}, u32[]{:S(2)}, u32[]{:S(2)}) async-start(bf16[32,2,648]{2,1,0:T(2,128)(2,1)} %reshape.265), calls=%async_computation.3 | async-start | bytes 196608 | tf_op jit(solution)/shard_map/all_to_all | solution.py:59
  414.8 56.4 %reduce-scatter.4.cloned.1.call-done = f32[336,1152]{1,0:T(8,128)} async-done(((f32[2688,1152]{1,0:T(8,128)}), f32[336,1152]{1,0:T(8,128)}) %reduce-scatter.4.cloned.1.call-update) | async-done | bytes 1548304
  471.2 2.6 reshape.249
  473.8 2.1 copy.37
  475.8 2.6 copy.29
  478.4 0.0 all-to-all-done.3
  478.4 8.1 %all-to-all-start.2 = ((bf16[336,288,4]{0,2,1:T(4,128)(2,1)}), bf16[336,288,4]{0,2,1:T(4,128)(2,1)S(1)}, u32[]{:S(2)}, u32[]{:S(2)}) async-start(bf16[336,288,4]{0,2,1:T(4,128)(2,1)} %copy.29), calls=%async_computation.2 | async-start | bytes 1769472 | tf_op jit(solution)/shard_map/all_to_all | solution.py:58
  486.5 0.4 reshape.266
  486.9 0.1 copy.33
  487.1 0.8 copy.35
  487.9 12.0 %all-to-all-done.2 = bf16[336,288,4]{0,2,1:T(4,128)(2,1)S(1)} async-done(((bf16[336,288,4]{0,2,1:T(4,128)(2,1)}), bf16[336,288,4]{0,2,1:T(4,128)(2,1)S(1)}, u32[]{:S(2)}, u32[]{:S(2)}) %all-to-all-start.2) | async-done | bytes 774176 | tf_op jit(solution)/shard_map/all_to_all | solution.py:58
  499.8 1.3 copy.30
  501.1 1.6 all_to_all.41
  502.7 1.5 copy.34
  (14 shorter events, 0.1 us)
Async XLA Ops:
  7.2 257.7 %copy-start = (bf16[384,2688]{1,0:T(8,128)(2,1)S(1)}, bf16[384,2688]{1,0:T(8,128)(2,1)}, u32[]{:S(2)}) copy-start(bf16[384,2688]{1,0:T(8,128)(2,1)} %param.13) | copy-start | bytes 6193156
  16.6 19.2 %all-to-all-start = ((s32[32,1,8]{2,1,0:T(1,128)}), s32[32,1,8]{2,1,0:T(1,128)S(1)}, u32[]{:S(2)}, u32[]{:S(2)}) async-start(s32[32,1,8]{2,1,0:T(1,128)} %bitcast.8), calls=%async_computation | async-start | bytes 32768 | tf_op jit(solution)/shard_map/all_to_all | solution.py:37
  35.8 7.9 %copy-start.3 = (s32[288]{0:T(512)S(1)}, s32[288]{0:T(512)}, u32[]{:S(2)}) copy-start(s32[288]{0:T(512)} %param.11) | copy-start | bytes 3460
  35.8 7.9 %copy-start.1 = (bf16[384,288]{0,1:T(8,128)(2,1)S(1)}, bf16[384,288]{0,1:T(8,128)(2,1)}, u32[]{:S(2)}) copy-start(bf16[384,288]{0,1:T(8,128)(2,1)} %param.12) | copy-start | bytes 663556
  35.8 109.0 %all-to-all-start.1 = ((bf16[32,8,128,128]{3,2,1,0:T(8,128)(2,1)}), bf16[32,8,128,128]{3,2,1,0:T(8,128)(2,1)}, u32[]{:S(2)}, u32[]{:S(2)}) async-start(bf16[32,8,128,128]{3,2,1,0:T(8,128)(2,1)} %bitcast.85), calls=%async_computation.1 | async-start | bytes 16777216 | tf_op jit(solution)/shard_map/all_to_all | solution.py:36
  43.6 214.2 %all-gather.3.cloned.1.call-start = ((), (), s32[]{:S(2)}) async-start(), calls=%async_computation.5 | async-start | bytes 1990656 | tf_op jit(solution)/shard_map/all_gather | solution.py:47
  46.2 425.0 %reduce-scatter.4.cloned.1.call-start = ((), (), s32[]{:S(2)}) async-start(), calls=%async_computation.6 | async-start | bytes 13934592
  306.2 0.7 copy-start.4
  306.2 1.9 copy-start.2
  405.8 72.6 %all-to-all-start.3 = ((bf16[32,2,648]{2,1,0:T(2,128)(2,1)}), bf16[32,2,648]{2,1,0:T(2,128)(2,1)S(1)}, u32[]{:S(2)}, u32[]{:S(2)}) async-start(bf16[32,2,648]{2,1,0:T(2,128)(2,1)} %reshape.265), calls=%async_computation.3 | async-start | bytes 196608 | tf_op jit(solution)/shard_map/all_to_all | solution.py:59
  478.4 21.4 %all-to-all-start.2 = ((bf16[336,288,4]{0,2,1:T(4,128)(2,1)}), bf16[336,288,4]{0,2,1:T(4,128)(2,1)S(1)}, u32[]{:S(2)}, u32[]{:S(2)}) async-start(bf16[336,288,4]{0,2,1:T(4,128)(2,1)} %copy.29), calls=%async_computation.2 | async-start | bytes 1769472 | tf_op jit(solution)/shard_map/all_to_all | solution.py:58
Sparse Core Ops, SparseCore 0:
  46.8 42.1 all-gather.2
  306.3 164.7 reduce-scatter.3
where the time goes:
time: 518 us; the launch traced here: 511 us
  waiting for transfers between devices  166 us (32%)
  local copies, waits for them, and re-layouts  113 us (22%)
  blocking collectives  90.8 us (18%)
  other arithmetic  78.2 us (15%)
  starting transfers between devices  32.3 us (6%)
  between operations  15.7 us (3%)
  matrix products  15.5 us (3%)
    all_to_all x1, waiting for transfers between devices, on_device(): lax.all_to_all(send_tiles, 'vec', split_axis=0, concat_axis=0, tiled=True)  97.2 us
    unnamed x1, blocking collectives  90.8 us
    unnamed x3, waiting for transfers between devices  56.4 us
    scatter-add x1, other arithmetic, on_device(): placed = jnp.zeros((dropped, tile_size, tile_size), jnp.float32).at[recv_...  51.9 us
    unnamed x19, local copies, waits for them, and re-layouts  44.5 us
    convert_element_type x2, local copies, waits for them, and re-layouts, on_device(): matrix.transpose(0, 1, 3, 2, 4).reshape(VEC_DEV, row_span, NAO)  29.5 us
    all_to_all x1, waiting for transfers between devices, on_device(): lax.all_to_all(ov_sum.astype(jnp.bfloat16), 'vec', split_axis=1, concat_a...  12 us
    gather x1, local copies, waits for them, and re-layouts, on_device(): send_tiles = blocks[source].reshape(owners, capacity, tile_size, tile_size)  11.8 us
  transfers between devices with their start and end apart: 6, of which 3 were waited for; matrix products, arithmetic and copies ran while one was open for 28% of the time, Pallas kernels for 0%

commit v1 on v0

v1 whole, which is shorter than its diff:
```python
import jax
import jax.numpy as jnp
from jax import lax
from jax.experimental import pallas as pl
from jax.experimental.pallas import tpu as pltpu
from jax.sharding import PartitionSpec as P

MESH = pl.DeviceIdType.MESH
F32, BF16, I32 = jnp.float32, jnp.bfloat16, jnp.int32

N_VEC, N_ROW, N_CHIP = 32, 8, 16
CAP, SLOTS, BLK = 8, 256, 128
NAO, NO, NV, SPAN = 3072, 288, 2688, 384
VEC_DEV, PAIRS, ACROSS, TALL = 4, 72, 24, 3
NV_R, NO_R, NO_V = NV // N_ROW, NO // N_ROW, NO // N_VEC
W_R = 384
WIDE = 4 * W_R
K_HALF = NO // 2
CHUNK = 32
PARTS = 8
Q = 8
VMEM = pltpu.VMEM
ANY = pl.BlockSpec(memory_space=pl.ANY)
IN_VMEM = pl.BlockSpec(memory_space=pltpu.VMEM)
DMA = pltpu.SemaphoreType.DMA


def prepare_kernel(vec_ref, pair_ref, count_ref, order_ref, occ_ref, vir_ref, blocks_ref,
                   send_ref, code_ref, w_ref, perm_ref, pos_vmem, pos_smem, sem, pos_sem):
    core = lax.rem(lax.axis_index("vec"), 2)
    count = count_ref[0, 0]
    vectors, pairs = vec_ref[...], pair_ref[...]
    owner = vectors // VEC_DEV
    code = vectors % VEC_DEV * PAIRS + pairs + 1
    above = lax.broadcasted_iota(I32, (SLOTS, SLOTS), 0)
    across = lax.broadcasted_iota(I32, (SLOTS, SLOTS), 1)
    owner_col = jnp.sum(jnp.where(above == across, owner, 0), axis=1, keepdims=True)
    earlier = (owner_col == owner) & (above < across)
    rank = jnp.sum(jnp.where(earlier, 1, 0), axis=0, keepdims=True)
    pos_vmem[...] = owner * CAP + rank
    to_smem = pltpu.make_async_copy(pos_vmem, pos_smem, pos_sem)
    to_smem.start()
    to_smem.wait()

    def begin(slot, carry):
        pltpu.make_async_copy(blocks_ref.at[slot], send_ref.at[pos_smem[0, slot]], sem).start()
        return carry

    lax.fori_loop(0, count, begin, 0)

    valid = lax.broadcasted_iota(I32, (1, SLOTS), 1) < count
    owners = lax.broadcasted_iota(I32, (N_VEC, SLOTS), 0)
    lane = lax.broadcasted_iota(I32, (N_VEC, BLK), 1)
    mine = (owners == owner) & valid
    table = jnp.zeros((N_VEC, BLK), I32)
    for r in range(CAP):
        picked = jnp.sum(jnp.where(mine & (rank == r), code, 0), axis=1, keepdims=True)
        table = jnp.where(lane == r, picked, table)
    code_ref[...] = jnp.broadcast_to(table[:, None, :], (N_VEC, 8, BLK))

    pick = (lax.broadcasted_iota(I32, (NO, NO), 0) == order_ref[...]).astype(BF16)
    perm = jnp.dot(occ_ref[...], pick, preferred_element_type=F32)
    perm_ref[...] = perm.T.astype(BF16)
    for half in range(2):
        @pl.when(core == half)
        def _():
            for q in range(4):
                r = 4 * half + q
                w_ref[:, 256 * q:256 * q + 256] = vir_ref[:, NV_R * r:NV_R * r + 256]
                tail = vir_ref[:, NV_R * r + 256:NV_R * r + NV_R].astype(F32)
                occ = perm[:, NO_R * r:NO_R * r + NO_R]
                zero = jnp.zeros((SPAN, 12), F32)
                w_ref[:, 1024 + 128 * q:1152 + 128 * q] = jnp.concatenate([tail, occ, zero], axis=1).astype(BF16)

    def end(slot, carry):
        pltpu.make_async_copy(blocks_ref.at[0], send_ref.at[0], sem).wait()
        return carry

    lax.fori_loop(0, count, end, 0)


def prepare(vectors, pairs, count, order, occ, vir, blocks):
    return pl.pallas_call(
        prepare_kernel,
        out_shape=(
            jax.ShapeDtypeStruct((N_VEC * CAP, BLK, BLK), BF16),
            jax.ShapeDtypeStruct((N_VEC, 8, BLK), I32),
            jax.ShapeDtypeStruct((SPAN, WIDE), BF16),
            jax.ShapeDtypeStruct((NO, SPAN), BF16),
        ),
        in_specs=[IN_VMEM, IN_VMEM, pl.BlockSpec(memory_space=pltpu.SMEM), IN_VMEM, IN_VMEM, IN_VMEM, ANY],
        out_specs=(ANY, IN_VMEM, IN_VMEM, IN_VMEM),
        scratch_shapes=[VMEM((1, SLOTS), I32), pltpu.SMEM((1, SLOTS), I32), DMA, DMA],
        compiler_params=pltpu.CompilerParams(vmem_limit_bytes=40 * 2**20),
        name="prepare",
    )(vectors, pairs, count, order, occ, vir, blocks)


def exchange_kernel(send, code, w, recv, rcode, wfull, lsem, tsend, trecv, csend, crecv, us, ur, ds, dr):
    v, z = lax.axis_index("vec"), lax.axis_index("row")
    core, x, y = lax.rem(v, 2), lax.rem(v // 2, 4), v // 8
    up, down = lax.rem(z + 1, N_ROW), lax.rem(z + N_ROW - 1, N_ROW)
    barrier = pltpu.get_barrier_semaphore()

    def greet(i, carry):
        pl.semaphore_signal(barrier, inc=1, device_id=(lax.rem(v + i, N_VEC), z), device_id_type=MESH)
        return carry

    lax.fori_loop(1, N_VEC, greet, 0)
    pl.semaphore_signal(barrier, inc=1, device_id=(v, up), device_id_type=MESH)
    pl.semaphore_signal(barrier, inc=1, device_id=(v, down), device_id_type=MESH)
    pl.semaphore_wait(barrier, N_VEC + 1)

    own = [
        pltpu.make_async_copy(send.at[v], recv.at[v], lsem.at[0]),
        pltpu.make_async_copy(code.at[v], rcode.at[v], lsem.at[1]),
        pltpu.make_async_copy(w, wfull.at[z], lsem.at[2]),
    ]
    for copy in own:
        copy.start()

    def remote(src, dst, send_sem, recv_sem, device):
        return pltpu.make_async_remote_copy(
            src_ref=src, dst_ref=dst, send_sem=send_sem, recv_sem=recv_sem, device_id=device, device_id_type=MESH
        )

    rows = SPAN // Q

    def ring(step, piece, sign):
        origin = lax.rem(z - sign * step + 2 * N_ROW, N_ROW)
        part = pl.ds(piece * rows, rows)
        src = w.at[part] if step == 0 else wfull.at[origin, part]
        ssem, rsem, to = (us, ur, up) if sign > 0 else (ds, dr, down)
        return remote(src, wfull.at[origin, part], ssem.at[step * Q + piece], rsem.at[step * Q + piece], (v, to))

    def pieces(step, sign):
        if step < 3:
            return 0, Q
        return (0, Q // 2) if sign > 0 else (Q // 2, Q)

    def first(piece, carry):
        ring(0, piece, 1).start()
        ring(0, piece, -1).start()
        return carry

    lax.fori_loop(0, Q, first, 0)

    def target(j):
        return ((y + j // 8) % 4) * 8 + ((x + j // 2) % 4) * 2 + lax.rem(core + j, 2)

    def give(n, carry):
        part = n // (N_VEC - 1)
        j = 1 + lax.rem(n * 11, N_VEC - 1)
        d = target(j)
        spot = pl.ds(part * (CAP // PARTS), CAP // PARTS)
        remote(send.at[d, spot], recv.at[v, spot], tsend.at[d], trecv.at[v], (d, z)).start()
        return carry

    def give_code(j, carry):
        d = target(j)
        remote(code.at[d], rcode.at[v], csend.at[d], crecv.at[v], (d, z)).start()
        return carry

    lax.fori_loop(0, PARTS * (N_VEC - 1), give, 0)
    lax.fori_loop(1, N_VEC, give_code, 0)

    for step in range(1, 4):
        for piece in range(Q):
            for sign in (1, -1):
                low, high = pieces(step, sign)
                if low <= piece < high:
                    ring(step - 1, piece, sign).wait_recv()
                    ring(step, piece, sign).start()

    def finish(i, carry):
        d = lax.rem(v + i, N_VEC)
        pltpu.make_async_copy(send.at[d], recv.at[d], tsend.at[d]).wait()
        pltpu.make_async_copy(code.at[d], rcode.at[d], csend.at[d]).wait()
        pltpu.make_async_copy(send.at[d], recv.at[d], trecv.at[d]).wait()
        pltpu.make_async_copy(code.at[d], rcode.at[d], crecv.at[d]).wait()
        return carry

    for sign in (1, -1):
        for step in range(4):
            low, high = pieces(step, sign)
            for piece in range(low, high):
                ring(step, piece, sign).wait_send()
        for step in (2, 3):
            low, high = pieces(step, sign)
            skip = pieces(3, sign) if step == 2 else (Q, Q)
            for piece in range(low, high):
                if not skip[0] <= piece < skip[1]:
                    ring(step, piece, sign).wait_recv()
    lax.fori_loop(1, N_VEC, finish, 0)
    for copy in own:
        copy.wait()


def exchange(send, code, w):
    return pl.pallas_call(
        exchange_kernel,
        out_shape=(
            jax.ShapeDtypeStruct(send.shape, BF16),
            jax.ShapeDtypeStruct(code.shape, I32),
            jax.ShapeDtypeStruct((N_ROW,) + w.shape, BF16),
        ),
        in_specs=[ANY] * 3,
        out_specs=(ANY,) * 3,
        scratch_shapes=[DMA((3,))] + [DMA((N_VEC,))] * 4 + [DMA((4 * Q,))] * 4,
        compiler_params=pltpu.CompilerParams(collective_id=0, has_side_effects=True),
        name="exchange",
    )(send, code, w)


def half_kernel(code_ref, tiles_ref, occ_ref, out_ref, tiles, dense, occ, sems):
    group = 32
    loads = [
        pltpu.make_async_copy(
            tiles_ref.at[pl.ds(n * group, group)], tiles.at[pl.ds(n * group, group)], sems.at[n]
        )
        for n in range(SLOTS // group)
    ]
    for load in loads:
        load.start()

    def clear(n, carry):
        dense[n] = jnp.zeros((BLK, NAO), F32)
        return carry

    lax.fori_loop(0, VEC_DEV * TALL, clear, 0)
    for r in range(N_ROW):
        occ[:, SPAN * r:SPAN * r + SPAN] = occ_ref[r]

    def place(n, carry):
        code = code_ref[n] - 1

        @pl.when(code >= 0)
        def _():
            block = code // ACROSS
            column = pl.ds(pl.multiple_of(lax.rem(code, ACROSS) * BLK, BLK), BLK)
            dense[block, :, column] += tiles[n].astype(F32)

        return carry

    for n, load in enumerate(loads):
        load.wait()
        lax.fori_loop(n * group, n * group + group, place, 0)

    for pair in range(VEC_DEV * TALL // 2):
        rows = jnp.concatenate([dense[2 * pair], dense[2 * pair + 1]], axis=0).astype(BF16)
        product = lax.dot_general(
            occ[...], rows, (((1,), (1,)), ((), ())), preferred_element_type=F32
        ).astype(BF16)
        for n in range(2):
            j, block = divmod(2 * pair + n, TALL)
            out_ref[j, :, BLK * block:BLK * block + BLK] = product[:, BLK * n:BLK * n + BLK]


def half_transform(code, tiles, occ):
    return pl.pallas_call(
        half_kernel,
        out_shape=jax.ShapeDtypeStruct((VEC_DEV, NO, SPAN), BF16),
        in_specs=[pl.BlockSpec(memory_space=pltpu.SMEM), ANY, IN_VMEM],
        out_specs=IN_VMEM,
        scratch_shapes=[
            VMEM((SLOTS, BLK, BLK), BF16),
            VMEM((VEC_DEV * TALL, BLK, NAO), F32),
            VMEM((NO, NAO), BF16),
            DMA((SLOTS // 32,)),
        ],
        compiler_params=pltpu.CompilerParams(vmem_limit_bytes=56 * 2**20),
        name="half",
    )(code, tiles, occ)


def finish_kernel(half, w_hbm, out_ref, w, held, total, chunk, taken, wide, wsem, lsem, hsend, hrecv, ssend, srecv, csend, crecv):
    v, z = lax.axis_index("vec"), lax.axis_index("row")
    chip, core = v // 2, lax.rem(v, 2)
    giver = z // 4
    takes_own = giver == core
    other = 2 * chip + 1 - core

    loads = [pltpu.make_async_copy(w_hbm.at[r], w.at[r], wsem.at[r]) for r in range(N_ROW)]
    for load in loads:
        load.start()

    barrier = pltpu.get_barrier_semaphore()

    def greet(device):
        pl.semaphore_signal(barrier, inc=1, device_id=device, device_id_type=MESH)

    def greet_sources(n, carry):
        source = (2 * (n // N_ROW) + giver, lax.rem(n, N_ROW))

        @pl.when(jnp.logical_not((source[0] == v) & (source[1] == z)))
        def _():
            greet(source)

        return carry

    lax.fori_loop(0, N_CHIP * N_ROW, greet_sources, 0)

    def greet_halves(r, carry):
        @pl.when(jnp.logical_not(takes_own & (r == z)))
        def _():
            greet((2 * chip + giver, r))

        return carry

    lax.fori_loop(0, N_ROW, greet_halves, 0)
    greet((other, z))
    expected = 8 + 1 + 4 * N_VEC - 2 * takes_own.astype(I32)
    pl.semaphore_wait(barrier, expected)

    def remote(src, dst, send_sem, recv_sem, device):
        return pltpu.make_async_remote_copy(
            src_ref=src, dst_ref=dst, send_sem=send_sem, recv_sem=recv_sem, device_id=device, device_id_type=MESH
        )

    def rows(h):
        return pl.ds(pl.multiple_of(h * K_HALF, 16), K_HALF)

    def send_half(n):
        j, h = n // 2, lax.rem(n, 2)
        return remote(half.at[j, rows(h)], held.at[z, rows(h)], hsend.at[n], hrecv.at[z], (2 * chip + h, 4 * core + j))

    def to_self(n):
        return (4 * core + n // 2 == z) & (lax.rem(n, 2) == core)

    stay = pltpu.make_async_copy(half.at[lax.rem(z, 4), rows(core)], held.at[z, rows(core)], lsem.at[0])

    def start_half(n, carry):
        @pl.when(jnp.logical_not(to_self(n)))
        def _():
            send_half(n).start()

        return carry

    lax.fori_loop(0, 8, start_half, 0)

    @pl.when(takes_own)
    def _():
        stay.start()

    def swap(r):
        return remote(held.at[r, rows(core)], held.at[r, rows(core)], ssend.at[r], srecv.at[r], (other, z))

    def pass_on(i):
        r = lax.rem(z + i, N_ROW)
        if i == 0:
            @pl.when(takes_own)
            def _():
                stay.wait()

            @pl.when(jnp.logical_not(takes_own))
            def _():
                pltpu.make_async_copy(held.at[r, rows(core)], held.at[r, rows(core)], hrecv.at[r]).wait()
        else:
            pltpu.make_async_copy(held.at[r, rows(core)], held.at[r, rows(core)], hrecv.at[r]).wait()
        swap(r).start()

    def arrived(i):
        r = lax.rem(z + i, N_ROW)
        theirs = held.at[r, rows(1 - core)]
        pltpu.make_async_copy(theirs, theirs, srecv.at[r]).wait()
        return r

    sequence = (0, 1, 7, 2, 6, 3, 5, 4)
    for load in loads:
        load.wait()
    for n in range(4):
        first, second = sequence[2 * n], sequence[2 * n + 1]
        pass_on(first)
        pass_on(second)
        a, b = arrived(first), arrived(second)
        deep = jnp.concatenate([held[a], held[b]], axis=1)
        for col in range(0, WIDE, 512):
            part = pl.ds(col, 512)
            block = jnp.concatenate([w[a, :, part], w[b, :, part]], axis=0)
            product = jnp.dot(deep, block, preferred_element_type=F32)
            if n == 0:
                total[:, part] = product
            else:
                total[:, part] += product

    row = lax.broadcasted_iota(I32, (N_VEC * CHUNK, NO), 0)
    source = lax.broadcasted_iota(I32, (N_VEC * CHUNK, NO), 1)
    inside = row % CHUNK
    base = row // CHUNK * NO_V
    stacked = jnp.zeros((N_VEC * CHUNK, 4 * BLK), F32)
    for t in range(3):
        pick = ((inside // NO_V == t) & (base + inside % NO_V == source)).astype(BF16)
        if t < 2:
            columns = jnp.concatenate([total[:, 256 * q + 128 * t:256 * q + 128 * t + 128] for q in range(4)], axis=1)
        else:
            columns = total[:, 1024:1536]
        stacked = stacked + jnp.dot(pick, columns.astype(BF16), preferred_element_type=F32)
    chunk[...] = stacked.astype(BF16)

    place = chip * N_ROW + z

    def final_copy(n):
        to, q = n // 4, lax.rem(n, 4)
        src = chunk.at[pl.ds(pl.multiple_of(to * CHUNK, CHUNK), CHUNK), pl.ds(pl.multiple_of(q * BLK, BLK), BLK)]
        dst = taken.at[pl.ds(pl.multiple_of(place * CHUNK, CHUNK), CHUNK)]
        return src, dst, (to, 4 * core + q)

    def start_final(i, carry):
        n = lax.rem(i * 37 + v * 4, 4 * N_VEC)
        src, dst, device = final_copy(n)
        own = (device[0] == v) & (device[1] == z)

        @pl.when(jnp.logical_not(own))
        def _():
            remote(src, dst, csend, crecv, device).start()

        @pl.when(own)
        def _():
            pltpu.make_async_copy(src, dst, lsem.at[1]).start()

        return carry

    lax.fori_loop(0, 4 * N_VEC, start_final, 0)

    def wait_half(n, carry):
        @pl.when(jnp.logical_not(to_self(n)))
        def _():
            send_half(n).wait_send()

        return carry

    lax.fori_loop(0, 8, wait_half, 0)

    def wait_swap(r, carry):
        swap(r).wait_send()
        return carry

    lax.fori_loop(0, N_ROW, wait_swap, 0)

    def wait_chunks(count):
        part = taken.at[pl.ds(0, count * CHUNK)]
        pltpu.make_async_copy(part, part, crecv).wait()
        pltpu.make_async_copy(part, part, csend).wait()

    @pl.when(takes_own)
    def _():
        wait_chunks(4 * N_VEC - 1)
        part = taken.at[pl.ds(0, CHUNK)]
        pltpu.make_async_copy(part, part, lsem.at[1]).wait()

    @pl.when(jnp.logical_not(takes_own))
    def _():
        wait_chunks(4 * N_VEC)

    wide[...] = taken[...].astype(F32)
    for t in range(3):
        for k in range(NO_V):
            block = wide[pl.ds(NO_V * t + k, BLK, stride=CHUNK), :]
            out_ref[k, BLK * t:BLK * t + BLK, :] = block.T.astype(BF16)


def finish(half, w):
    return pl.pallas_call(
        finish_kernel,
        out_shape=jax.ShapeDtypeStruct((NO_V, W_R, BLK), BF16),
        in_specs=[IN_VMEM, ANY],
        out_specs=IN_VMEM,
        scratch_shapes=[
            VMEM((N_ROW, SPAN, WIDE), BF16),
            VMEM((N_ROW, NO, SPAN), BF16),
            VMEM((NO, WIDE), F32),
            VMEM((N_VEC * CHUNK, 4 * BLK), BF16),
            VMEM((BLK * CHUNK, BLK), BF16),
            VMEM((BLK * CHUNK, BLK), F32),
            DMA((N_ROW,)),
            DMA((2,)),
            DMA((8,)),
            DMA((N_ROW,)),
            DMA((N_ROW,)),
            DMA((N_ROW,)),
            DMA,
            DMA,
        ],
        compiler_params=pltpu.CompilerParams(
            collective_id=1, has_side_effects=True, vmem_limit_bytes=48 * 2**20
        ),
        name="finish",
    )(half, w)


def on_device(blocks, block_vector, block_pair, block_count, occ_order, occ_coeffs, vir_coeffs):
    send, code, w, perm = prepare(
        block_vector, block_pair, block_count, occ_order.reshape(1, NO), occ_coeffs, vir_coeffs, blocks
    )
    occ = lax.all_gather(perm, "row", axis=0)
    tiles, codes, w_all = exchange(send.reshape(N_VEC, CAP, BLK, BLK), code, w)
    half = half_transform(codes[:, 0, :CAP].reshape(-1), tiles.reshape(SLOTS, BLK, BLK), occ)
    result = finish(half, w_all)
    return (
        result[:, :NV_R].transpose(1, 0, 2),
        result[:, NV_R:NV_R + NO_R].transpose(1, 0, 2),
    )


def solution(mesh):
    placed = (
        P("vec", "row", None),
        P("row", "vec"),
        P("row", "vec"),
        P("row", "vec"),
        P(),
        P("row", None),
        P("row", None),
    )
    return jax.shard_map(
        on_device,
        mesh=mesh,
        in_specs=placed,
        out_specs=(P("row", "vec", None), P("row", "vec", None)),
        check_vma=False,
    )
```

time: 518 us -> 233 us (0.45)
  Pallas kernels: 0 us -> 202 us
  waiting for transfers between devices: 166 us -> 0.02 us
  local copies, waits for them, and re-layouts: 113 us -> 14.1 us
  blocking collectives: 90.8 us -> 0 us
  other arithmetic: 78.2 us -> 0 us
  starting transfers between devices: 32.3 us -> 0.04 us
  matrix products: 15.5 us -> 0 us
    pallas_call x0 -> x4, Pallas kernels: none -> 202 us  [the longest x1 116 us: exchange(): pl.pallas_call(exchange_kernel, out_shape=(jax.ShapeDtypeStruct(send.shap...]
    all_to_all x4 -> x0, waiting for transfers between devices: 109 us -> none  [the longest x1 97.2 us: on_device(): lax.all_to_all(send_tiles, 'vec', split_axis=0, concat_axis=0, tiled=True)]
    unnamed x1 -> x0, blocking collectives: 90.8 us -> none
    unnamed x3 -> x1, waiting for transfers between devices: 56.4 us -> 0.02 us
    scatter-add x1 -> x0, other arithmetic: 51.9 us -> none  [on_device(): placed = jnp.zeros((dropped, tile_size, tile_size), jnp.float32).at[recv_...]
    unnamed x19 -> x15, local copies, waits for them, and re-layouts: 44.5 us -> 10.2 us
    convert_element_type x5 -> x0, local copies, waits for them, and re-layouts: 32.4 us -> none  [the longest x2 29.5 us: on_device(): matrix.transpose(0, 1, 3, 2, 4).reshape(VEC_DEV, row_span, NAO)]
    all_to_all x4 -> x0, starting transfers between devices: 32.2 us -> none  [the longest x1 9.01 us: on_device(): lax.all_to_all(oo_sum.astype(jnp.bfloat16), 'vec', split_axis=1, concat_a...]
  transfers between devices with their start and end apart: 6 -> 1, of which waited for: 3 -> 0; matrix products, arithmetic and copies ran while one was open for 28% -> 1% of each run, Pallas kernels for 0% -> 50%
where the time goes in v1:
time: 233 us; the launch traced here: 230 us
  Pallas kernels  202 us (87%)
  between operations  14.7 us (6%)
  local copies, waits for them, and re-layouts  14.1 us (6%)
    pallas_call x1, Pallas kernels, exchange(): pl.pallas_call(exchange_kernel, out_shape=(jax.ShapeDtypeStruct(send.shap...  116 us
    pallas_call x1, Pallas kernels, finish(): pl.pallas_call(finish_kernel, out_shape=jax.ShapeDtypeStruct((NO_V, W_R,...  71.1 us
    pallas_call x1, Pallas kernels, half_transform(): pl.pallas_call(half_kernel, out_shape=jax.ShapeDtypeStruct((VEC_DEV, NO,...  11.9 us
    unnamed x15, local copies, waits for them, and re-layouts  10.2 us
  transfers between devices with their start and end apart: 1, of which 0 were waited for; matrix products, arithmetic and copies ran while one was open for 1% of the time, Pallas kernels for 50%

profile of v1, /device:TPU:56, one launch (start us, length us, event | category | flops | bytes accessed | tf_op | source)
XLA Modules:
  0.0 230.4 jit_solution(11160757629261616017)
XLA Ops:
  7.2 0.0 all-gather.3.cloned.1.call-start
  7.2 1.1 copy.10.occ_ref
  8.4 0.7 reshape.13.order_ref
  9.7 0.0 copy-start.2
  9.7 1.6 copy-done.2
  11.3 0.0 copy-start.5
  11.3 0.7 copy-done.5
  12.0 0.0 copy-start.6
  12.0 0.7 copy-done.6
  12.6 2.8 %prepare.1 = (bf16[256,128,128]{2,1,0:T(8,128)(2,1)S(1)}, s32[32,8,128]{2,1,0:T(8,128)S(1)}, bf16[384,1536]{1,0:T(8,128)(2,1)S(1)}, bf16[288,384]{1,0:T(8,128)(2,1)}) custom-call(s32[1,256]{1,0:T(1,128)S(1)} %copy-done.5, s32[1,256]{1,0:T(1,128)S(1)} %copy-done.6, s32[1,1]{1,0:T(1,128)S(6)} %copy.11.count_ref, s32[1,288]{1,0:T(1,128)S(1)} %reshape.13.order_ref, ...), custom_call_target="tpu_custom_call" | custom-call | tf_op jit(solution)/shard_map/prepare/pallas_call | solution.py:83
  15.4 0.0 copy-start
  15.4 3.3 %copy-done = bf16[256,128,128]{2,1,0:T(8,128)(2,1)} copy-done((bf16[256,128,128]{2,1,0:T(8,128)(2,1)}, bf16[256,128,128]{2,1,0:T(8,128)(2,1)S(1)}, u32[]{:S(2)}) %copy-start) | copy-done | bytes 8388632
  18.7 0.0 copy-start.3
  18.7 1.0 copy-done.3
  19.8 0.0 copy-start.4
  19.8 0.6 copy-done.4
  20.4 0.0 all-gather.3.cloned.1.call-update
  20.4 115.8 %exchange.1 = (bf16[32,8,128,128]{3,2,1,0:T(8,128)(2,1)}, s32[32,8,128]{2,1,0:T(8,128)}, bf16[8,384,1536]{2,1,0:T(8,128)(2,1)}) custom-call(bf16[32,8,128,128]{3,2,1,0:T(8,128)(2,1)} %bitcast.7, s32[32,8,128]{2,1,0:T(8,128)} %copy-done.4, bf16[384,1536]{1,0:T(8,128)(2,1)} %copy-done.3), custom_call_target="tpu_custom_call" | custom-call | tf_op jit(solution)/shard_map/exchange/pallas_call | solution.py:200
  136.3 0.9 slice_reduce_fusion
  137.2 0.7 reshape_squeeze.3.code_ref
  137.9 0.0 all-gather.3.cloned.1.call-done
  137.9 11.9 %half.1 = bf16[4,288,384]{2,1,0:T(8,128)(2,1)} custom-call(s32[256]{0:T(256)} %reshape_squeeze.3.code_ref, bf16[256,128,128]{2,1,0:T(8,128)(2,1)} %bitcast.8, bf16[8,288,384]{2,1,0:T(8,128)(2,1)} %bitcast.9), custom_call_target="tpu_custom_call" | custom-call | tf_op jit(solution)/shard_map/half/pallas_call | solution.py:260
  149.8 0.0 copy-start.1
  149.8 1.2 copy-done.1
  150.9 71.1 %finish.1 = bf16[9,384,128]{2,1,0:T(8,128)(2,1)S(1)} custom-call(bf16[4,288,384]{2,1,0:T(8,128)(2,1)S(1)} %copy-done.1, bf16[8,384,1536]{2,1,0:T(8,128)(2,1)} %get-tuple-element.15.w_hbm), custom_call_target="tpu_custom_call" | custom-call | tf_op jit(solution)/shard_map/finish/pallas_call | solution.py:463
  222.0 0.9 slice_bitcast_fusion
  222.9 0.6 slice_bitcast_fusion.1
Async XLA Ops:
  7.2 130.7 %all-gather.3.cloned.1.call-start = ((), (), s32[]{:S(2)}) async-start(), calls=%async_computation | async-start | bytes 1990656 | tf_op jit(solution)/shard_map/all_gather | solution.py:495
  9.7 1.6 copy-start.2
  11.3 0.7 copy-start.5
  12.0 0.7 copy-start.6
  15.4 3.3 %copy-start = (bf16[256,128,128]{2,1,0:T(8,128)(2,1)}, bf16[256,128,128]{2,1,0:T(8,128)(2,1)S(1)}, u32[]{:S(2)}) copy-start(bf16[256,128,128]{2,1,0:T(8,128)(2,1)S(1)} %get-tuple-element.9) | copy-start | bytes 25165828
  18.7 1.0 copy-start.3
  19.8 0.6 copy-start.4
  149.8 1.2 copy-start.1
Sparse Core Ops, SparseCore 0:
  20.5 58.0 all-gather.2

commit v2 on v1

--- a/solution.py
+++ b/solution.py
@@ -20,18 +20,28 @@
 PARTS = 8
 Q = 8
 VMEM = pltpu.VMEM
+LIMIT = 60 * 2**20
 ANY = pl.BlockSpec(memory_space=pl.ANY)
 IN_VMEM = pl.BlockSpec(memory_space=pltpu.VMEM)
 DMA = pltpu.SemaphoreType.DMA
 
 
-def prepare_kernel(vec_ref, pair_ref, count_ref, order_ref, occ_ref, vir_ref, blocks_ref,
-                   send_ref, code_ref, w_ref, perm_ref, pos_vmem, pos_smem, sem, pos_sem):
+def prepare_kernel(vec_hbm, pair_hbm, count_ref, order_hbm, occ_hbm, vir_hbm, blocks_ref,
+                   send_ref, code_hbm, w_hbm, vec_ref, pair_ref, order_ref, occ_ref, vir_ref,
+                   code_ref, w_ref, pos_vmem, pos_smem, sem, pos_sem, in_sems, out_sems):
+    loads = [
+        pltpu.make_async_copy(src, dst, in_sems.at[n])
+        for n, (src, dst) in enumerate(
+            ((vec_hbm, vec_ref), (pair_hbm, pair_ref), (order_hbm, order_ref), (occ_hbm, occ_ref), (vir_hbm, vir_ref))
+        )
+    ]
+    for load in loads:
+        load.start()
     core = lax.rem(lax.axis_index("vec"), 2)
     count = count_ref[0, 0]
-    vectors, pairs = vec_ref[...], pair_ref[...]
+    loads[0].wait()
+    vectors = vec_ref[...]
     owner = vectors // VEC_DEV
-    code = vectors % VEC_DEV * PAIRS + pairs + 1
     above = lax.broadcasted_iota(I32, (SLOTS, SLOTS), 0)
     across = lax.broadcasted_iota(I32, (SLOTS, SLOTS), 1)
     owner_col = jnp.sum(jnp.where(above == across, owner, 0), axis=1, keepdims=True)
@@ -48,6 +58,8 @@
 
     lax.fori_loop(0, count, begin, 0)
 
+    loads[1].wait()
+    code = vectors % VEC_DEV * PAIRS + pair_ref[...] + 1
     valid = lax.broadcasted_iota(I32, (1, SLOTS), 1) < count
     owners = lax.broadcasted_iota(I32, (N_VEC, SLOTS), 0)
     lane = lax.broadcasted_iota(I32, (N_VEC, BLK), 1)
@@ -57,10 +69,13 @@
         picked = jnp.sum(jnp.where(mine & (rank == r), code, 0), axis=1, keepdims=True)
         table = jnp.where(lane == r, picked, table)
     code_ref[...] = jnp.broadcast_to(table[:, None, :], (N_VEC, 8, BLK))
-
+    code_out = pltpu.make_async_copy(code_ref, code_hbm, out_sems.at[0])
+    code_out.start()
+
+    for load in loads[2:]:
+        load.wait()
     pick = (lax.broadcasted_iota(I32, (NO, NO), 0) == order_ref[...]).astype(BF16)
-    perm = jnp.dot(occ_ref[...], pick, preferred_element_type=F32)
-    perm_ref[...] = perm.T.astype(BF16)
+    perm = lax.dot_general(occ_ref[...], pick, (((0,), (0,)), ((), ())), preferred_element_type=F32)
     for half in range(2):
         @pl.when(core == half)
         def _():
@@ -71,12 +86,16 @@
                 occ = perm[:, NO_R * r:NO_R * r + NO_R]
                 zero = jnp.zeros((SPAN, 12), F32)
                 w_ref[:, 1024 + 128 * q:1152 + 128 * q] = jnp.concatenate([tail, occ, zero], axis=1).astype(BF16)
+    w_out = pltpu.make_async_copy(w_ref, w_hbm, out_sems.at[1])
+    w_out.start()
 
     def end(slot, carry):
         pltpu.make_async_copy(blocks_ref.at[0], send_ref.at[0], sem).wait()
         return carry
 
     lax.fori_loop(0, count, end, 0)
+    code_out.wait()
+    w_out.wait()
 
 
 def prepare(vectors, pairs, count, order, occ, vir, blocks):
@@ -86,17 +105,30 @@
             jax.ShapeDtypeStruct((N_VEC * CAP, BLK, BLK), BF16),
             jax.ShapeDtypeStruct((N_VEC, 8, BLK), I32),
             jax.ShapeDtypeStruct((SPAN, WIDE), BF16),
-            jax.ShapeDtypeStruct((NO, SPAN), BF16),
         ),
-        in_specs=[IN_VMEM, IN_VMEM, pl.BlockSpec(memory_space=pltpu.SMEM), IN_VMEM, IN_VMEM, IN_VMEM, ANY],
-        out_specs=(ANY, IN_VMEM, IN_VMEM, IN_VMEM),
-        scratch_shapes=[VMEM((1, SLOTS), I32), pltpu.SMEM((1, SLOTS), I32), DMA, DMA],
-        compiler_params=pltpu.CompilerParams(vmem_limit_bytes=40 * 2**20),
+        in_specs=[ANY, ANY, pl.BlockSpec(memory_space=pltpu.SMEM), ANY, ANY, ANY, ANY],
+        out_specs=(ANY, ANY, ANY),
+        scratch_shapes=[
+            VMEM((1, SLOTS), I32),
+            VMEM((1, SLOTS), I32),
+            VMEM((1, NO), I32),
+            VMEM((NO, SPAN), BF16),
+            VMEM((SPAN, NV), BF16),
+            VMEM((N_VEC, 8, BLK), I32),
+            VMEM((SPAN, WIDE), BF16),
+            VMEM((1, SLOTS), I32),
+            pltpu.SMEM((1, SLOTS), I32),
+            DMA,
+            DMA,
+            DMA((5,)),
+            DMA((2,)),
+        ],
+        compiler_params=pltpu.CompilerParams(vmem_limit_bytes=LIMIT),
         name="prepare",
     )(vectors, pairs, count, order, occ, vir, blocks)
 
 
-def exchange_kernel(send, code, w, recv, rcode, wfull, lsem, tsend, trecv, csend, crecv, us, ur, ds, dr):
+def exchange_kernel(send, code, w, recv, rcode, wfull, theirs, lsem, tsend, trecv, csend, crecv, us, ur, ds, dr, os, orc):
     v, z = lax.axis_index("vec"), lax.axis_index("row")
     core, x, y = lax.rem(v, 2), lax.rem(v // 2, 4), v // 8
     up, down = lax.rem(z + 1, N_ROW), lax.rem(z + N_ROW - 1, N_ROW)
@@ -124,6 +156,10 @@
             src_ref=src, dst_ref=dst, send_sem=send_sem, recv_sem=recv_sem, device_id=device, device_id_type=MESH
         )
 
+    def swap(origin, src):
+        columns = pl.ds(1024, 512)
+        return remote(src.at[:, columns], theirs.at[origin], os.at[origin], orc.at[origin], (v + 1 - 2 * core, z))
+
     rows = SPAN // Q
 
     def ring(step, piece, sign):
@@ -144,6 +180,7 @@
         return carry
 
     lax.fori_loop(0, Q, first, 0)
+    swap(z, w).start()
 
     def target(j):
         return ((y + j // 8) % 4) * 8 + ((x + j // 2) % 4) * 2 + lax.rem(core + j, 2)
@@ -163,6 +200,10 @@
 
     lax.fori_loop(0, PARTS * (N_VEC - 1), give, 0)
     lax.fori_loop(1, N_VEC, give_code, 0)
+
+    def pass_occ(step, sign):
+        origin = lax.rem(z - sign * step + N_ROW, N_ROW)
+        swap(origin, wfull.at[origin]).start()
 
     for step in range(1, 4):
         for piece in range(Q):
@@ -171,6 +212,9 @@
                 if low <= piece < high:
                     ring(step - 1, piece, sign).wait_recv()
                     ring(step, piece, sign).start()
+        if step < 3:
+            pass_occ(step, 1)
+            pass_occ(step, -1)
 
     def finish(i, carry):
         d = lax.rem(v + i, N_VEC)
@@ -181,16 +225,24 @@
         return carry
 
     for sign in (1, -1):
+        low, high = pieces(3, sign)
+        for piece in range(Q):
+            if not low <= piece < high:
+                ring(2, piece, sign).wait_recv()
+        pass_occ(3, sign)
+    for sign in (1, -1):
+        low, high = pieces(3, sign)
+        for piece in range(low, high):
+            ring(3, piece, sign).wait_recv()
+    pass_occ(4, 1)
+    for sign in (1, -1):
         for step in range(4):
             low, high = pieces(step, sign)
             for piece in range(low, high):
                 ring(step, piece, sign).wait_send()
-        for step in (2, 3):
-            low, high = pieces(step, sign)
-            skip = pieces(3, sign) if step == 2 else (Q, Q)
-            for piece in range(low, high):
-                if not skip[0] <= piece < skip[1]:
-                    ring(step, piece, sign).wait_recv()
+    for origin in range(N_ROW):
+        pltpu.make_async_copy(theirs.at[origin], theirs.at[origin], os.at[origin]).wait()
+        pltpu.make_async_copy(theirs.at[origin], theirs.at[origin], orc.at[origin]).wait()
     lax.fori_loop(1, N_VEC, finish, 0)
     for copy in own:
         copy.wait()
@@ -203,17 +255,26 @@
             jax.ShapeDtypeStruct(send.shape, BF16),
             jax.ShapeDtypeStruct(code.shape, I32),
             jax.ShapeDtypeStruct((N_ROW,) + w.shape, BF16),
+            jax.ShapeDtypeStruct((N_ROW, SPAN, 512), BF16),
         ),
         in_specs=[ANY] * 3,
-        out_specs=(ANY,) * 3,
-        scratch_shapes=[DMA((3,))] + [DMA((N_VEC,))] * 4 + [DMA((4 * Q,))] * 4,
-        compiler_params=pltpu.CompilerParams(collective_id=0, has_side_effects=True),
+        out_specs=(ANY,) * 4,
+        scratch_shapes=[DMA((3,))] + [DMA((N_VEC,))] * 4 + [DMA((4 * Q,))] * 4 + [DMA((N_ROW,))] * 2,
+        compiler_params=pltpu.CompilerParams(collective_id=0, has_side_effects=True, vmem_limit_bytes=LIMIT),
         name="exchange",
     )(send, code, w)
 
 
-def half_kernel(code_ref, tiles_ref, occ_ref, out_ref, tiles, dense, occ, sems):
+def half_kernel(code_hbm, tiles_ref, w_hbm, theirs_hbm, out_ref, tiles, dense, occ, own, theirs, code_ref, sems, more):
     group = 32
+    core = lax.rem(lax.axis_index("vec"), 2)
+    others = [
+        pltpu.make_async_copy(code_hbm, code_ref, more.at[0]),
+        pltpu.make_async_copy(w_hbm.at[:, :, pl.ds(1024, 512)], own, more.at[1]),
+        pltpu.make_async_copy(theirs_hbm, theirs, more.at[2]),
+    ]
+    for load in others:
+        load.start()
     loads = [
         pltpu.make_async_copy(
             tiles_ref.at[pl.ds(n * group, group)], tiles.at[pl.ds(n * group, group)], sems.at[n]
@@ -228,11 +289,24 @@
         return carry
 
     lax.fori_loop(0, VEC_DEV * TALL, clear, 0)
+    for load in others:
+        load.wait()
+    index = lax.broadcasted_iota(I32, (NO, 512), 0)
+    column = lax.broadcasted_iota(I32, (NO, 512), 1)
+    lane = column % BLK - (NV_R - 256)
+    found = (lane >= 0) & (lane < NO_R)
+    wanted = index - NO_R * (column // BLK) - lane
+    pick_own = (found & (wanted == 4 * NO_R * core)).astype(BF16)
+    pick_theirs = (found & (wanted == 4 * NO_R * (1 - core))).astype(BF16)
+    across = (((1,), (1,)), ((), ()))
     for r in range(N_ROW):
-        occ[:, SPAN * r:SPAN * r + SPAN] = occ_ref[r]
+        occ[:, SPAN * r:SPAN * r + SPAN] = (
+            lax.dot_general(pick_own, own[r], across, preferred_element_type=F32)
+            + lax.dot_general(pick_theirs, theirs[r], across, preferred_element_type=F32)
+        ).astype(BF16)
 
     def place(n, carry):
-        code = code_ref[n] - 1
+        code = code_ref[n // CAP, 0, lax.rem(n, CAP)] - 1
 
         @pl.when(code >= 0)
         def _():
@@ -256,24 +330,28 @@
             out_ref[j, :, BLK * block:BLK * block + BLK] = product[:, BLK * n:BLK * n + BLK]
 
 
-def half_transform(code, tiles, occ):
+def half_transform(code, tiles, w, theirs):
     return pl.pallas_call(
         half_kernel,
         out_shape=jax.ShapeDtypeStruct((VEC_DEV, NO, SPAN), BF16),
-        in_specs=[pl.BlockSpec(memory_space=pltpu.SMEM), ANY, IN_VMEM],
+        in_specs=[ANY] * 4,
         out_specs=IN_VMEM,
         scratch_shapes=[
             VMEM((SLOTS, BLK, BLK), BF16),
             VMEM((VEC_DEV * TALL, BLK, NAO), F32),
             VMEM((NO, NAO), BF16),
+            VMEM((N_ROW, SPAN, 512), BF16),
+            VMEM((N_ROW, SPAN, 512), BF16),
+            pltpu.SMEM((N_VEC, 8, BLK), I32),
             DMA((SLOTS // 32,)),
+            DMA((3,)),
         ],
-        compiler_params=pltpu.CompilerParams(vmem_limit_bytes=56 * 2**20),
+        compiler_params=pltpu.CompilerParams(vmem_limit_bytes=LIMIT),
         name="half",
-    )(code, tiles, occ)
-
-
-def finish_kernel(half, w_hbm, out_ref, w, held, total, chunk, taken, wide, wsem, lsem, hsend, hrecv, ssend, srecv, csend, crecv):
+    )(code, tiles, w, theirs)
+
+
+def finish_kernel(half, w_hbm, out_ref, w, held, total, chunk, taken, wide, wsem, lsem, hsend, hrecv, ssend, srecv, csend, crecv, x_sem, y_sem):
     v, z = lax.axis_index("vec"), lax.axis_index("row")
     chip, core = v // 2, lax.rem(v, 2)
     giver = z // 4
@@ -289,28 +367,30 @@
     def greet(device):
         pl.semaphore_signal(barrier, inc=1, device_id=device, device_id_type=MESH)
 
-    def greet_sources(n, carry):
-        source = (2 * (n // N_ROW) + giver, lax.rem(n, N_ROW))
-
-        @pl.when(jnp.logical_not((source[0] == v) & (source[1] == z)))
-        def _():
-            greet(source)
-
-        return carry
-
-    lax.fori_loop(0, N_CHIP * N_ROW, greet_sources, 0)
-
-    def greet_halves(r, carry):
-        @pl.when(jnp.logical_not(takes_own & (r == z)))
-        def _():
-            greet((2 * chip + giver, r))
-
-        return carry
-
-    lax.fori_loop(0, N_ROW, greet_halves, 0)
-    greet((other, z))
-    expected = 8 + 1 + 4 * N_VEC - 2 * takes_own.astype(I32)
-    pl.semaphore_wait(barrier, expected)
+    x, y = lax.rem(chip, 4), chip // 4
+
+    def line(i, carry):
+        greet((v, lax.rem(z + i, N_ROW)))
+        return carry
+
+    def other_line(i, carry):
+        greet((other, lax.rem(z + i, N_ROW)))
+        return carry
+
+    def along_x(i):
+        return (y * 8 + lax.rem(x + i, 4) * 2 + core, z)
+
+    def along_y(i):
+        return (lax.rem(y + i, 4) * 8 + x * 2 + core, z)
+
+    lax.fori_loop(1, N_ROW, line, 0)
+    lax.fori_loop(0, N_ROW, other_line, 0)
+    for i in range(1, 4):
+        greet(along_x(i))
+        greet(along_y(i))
+    pl.semaphore_wait(barrier, 7 + 8 + 6)
+    for i in range(1, 4):
+        pl.semaphore_signal(x_sem, inc=1, device_id=along_x(i), device_id_type=MESH)
 
     def remote(src, dst, send_sem, recv_sem, device):
         return pltpu.make_async_remote_copy(
@@ -364,6 +444,10 @@
         theirs = held.at[r, rows(1 - core)]
         pltpu.make_async_copy(theirs, theirs, srecv.at[r]).wait()
         return r
+
+    pl.semaphore_wait(x_sem, 3)
+    for i in range(1, 4):
+        pl.semaphore_signal(y_sem, inc=1, device_id=along_y(i), device_id_type=MESH)
 
     sequence = (0, 1, 7, 2, 6, 3, 5, 4)
     for load in loads:
@@ -395,13 +479,15 @@
         else:
             columns = total[:, 1024:1536]
         stacked = stacked + jnp.dot(pick, columns.astype(BF16), preferred_element_type=F32)
-    chunk[...] = stacked.astype(BF16)
+    for q in range(4):
+        chunk[q] = stacked[:, BLK * q:BLK * q + BLK].astype(BF16)
+    pl.semaphore_wait(y_sem, 3)
 
     place = chip * N_ROW + z
 
     def final_copy(n):
         to, q = n // 4, lax.rem(n, 4)
-        src = chunk.at[pl.ds(pl.multiple_of(to * CHUNK, CHUNK), CHUNK), pl.ds(pl.multiple_of(q * BLK, BLK), BLK)]
+        src = chunk.at[q, pl.ds(pl.multiple_of(to * CHUNK, CHUNK), CHUNK)]
         dst = taken.at[pl.ds(pl.multiple_of(place * CHUNK, CHUNK), CHUNK)]
         return src, dst, (to, 4 * core + q)
 
@@ -463,13 +549,13 @@
     return pl.pallas_call(
         finish_kernel,
         out_shape=jax.ShapeDtypeStruct((NO_V, W_R, BLK), BF16),
-        in_specs=[IN_VMEM, ANY],
+        in_specs=[ANY, ANY],
         out_specs=IN_VMEM,
         scratch_shapes=[
             VMEM((N_ROW, SPAN, WIDE), BF16),
             VMEM((N_ROW, NO, SPAN), BF16),
             VMEM((NO, WIDE), F32),
-            VMEM((N_VEC * CHUNK, 4 * BLK), BF16),
+            VMEM((4, N_VEC * CHUNK, BLK), BF16),
             VMEM((BLK * CHUNK, BLK), BF16),
             VMEM((BLK * CHUNK, BLK), F32),
             DMA((N_ROW,)),
@@ -480,21 +566,22 @@
             DMA((N_ROW,)),
             DMA,
             DMA,
+            pltpu.SemaphoreType.REGULAR,
+            pltpu.SemaphoreType.REGULAR,
         ],
         compiler_params=pltpu.CompilerParams(
-            collective_id=1, has_side_effects=True, vmem_limit_bytes=48 * 2**20
+            collective_id=1, has_side_effects=True, vmem_limit_bytes=LIMIT
         ),
         name="finish",
     )(half, w)
 
 
 def on_device(blocks, block_vector, block_pair, block_count, occ_order, occ_coeffs, vir_coeffs):
-    send, code, w, perm = prepare(
-        block_vector, block_pair, block_count, occ_order.reshape(1, NO), occ_coeffs, vir_coeffs, blocks
+    send, code, w = prepare(
+        block_vector, block_pair, block_count, occ_order.reshape(1, NO), occ_coeffs.T, vir_coeffs, blocks
     )
-    occ = lax.all_gather(perm, "row", axis=0)
-    tiles, codes, w_all = exchange(send.reshape(N_VEC, CAP, BLK, BLK), code, w)
-    half = half_transform(codes[:, 0, :CAP].reshape(-1), tiles.reshape(SLOTS, BLK, BLK), occ)
+    tiles, codes, w_all, theirs = exchange(send.reshape(N_VEC, CAP, BLK, BLK), code, w)
+    half = half_transform(codes, tiles.reshape(SLOTS, BLK, BLK), w_all, theirs)
     result = finish(half, w_all)
     return (
         result[:, :NV_R].transpose(1, 0, 2),

time: 233 us -> 452 us (1.94)
  Pallas kernels: 202 us -> 444 us
  between operations: 14.7 us -> 1.31 us
  local copies, waits for them, and re-layouts: 14.1 us -> 4.84 us
    pallas_call x1, Pallas kernels: 116 us -> 319 us  [exchange(): pl.pallas_call(exchange_kernel, out_shape=(jax.ShapeDtypeStruct(send.shap...]
    pallas_call x1, Pallas kernels: 2.77 us -> 37.3 us  [prepare(): pl.pallas_call(prepare_kernel, out_shape=(jax.ShapeDtypeStruct((N_VEC * C...]
    unnamed x15 -> x0, local copies, waits for them, and re-layouts: 10.2 us -> none
    pallas_call x1, Pallas kernels: 11.9 us -> 18.6 us  [half_transform(): pl.pallas_call(half_kernel, out_shape=jax.ShapeDtypeStruct((VEC_DEV, NO,...]
  transfers between devices with their start and end apart: 1 -> 0, of which waited for: 0 -> 0; matrix products, arithmetic and copies ran while one was open for 1% -> 0% of each run, Pallas kernels for 50% -> 0%
where the time goes in v2:
time: 452 us; the launch traced here: 450 us
  Pallas kernels  444 us (98%)
  local copies, waits for them, and re-layouts  4.84 us (1%)
    pallas_call x1, Pallas kernels, exchange(): pl.pallas_call(exchange_kernel, out_shape=(jax.ShapeDtypeStruct(send.shap...  319 us
    pallas_call x1, Pallas kernels, finish(): pl.pallas_call(finish_kernel, out_shape=jax.ShapeDtypeStruct((NO_V, W_R,...  68.7 us
    pallas_call x1, Pallas kernels, prepare(): pl.pallas_call(prepare_kernel, out_shape=(jax.ShapeDtypeStruct((N_VEC * C...  37.3 us
    pallas_call x1, Pallas kernels, half_transform(): pl.pallas_call(half_kernel, out_shape=jax.ShapeDtypeStruct((VEC_DEV, NO,...  18.6 us

profile of v2, /device:TPU:56, one launch (start us, length us, event | category | flops | bytes accessed | tf_op | source)
XLA Modules:
  0.0 449.8 jit_solution(14720298648610041963)
XLA Ops:
  1.3 1.2 reshape.13.order_hbm
  2.5 37.3 %prepare.1 = (bf16[256,128,128]{2,1,0:T(8,128)(2,1)}, s32[32,8,128]{2,1,0:T(8,128)}, bf16[384,1536]{1,0:T(8,128)(2,1)}) custom-call(s32[1,256]{1,0:T(1,128)} %vec_hbm.1, s32[1,256]{1,0:T(1,128)} %pair_hbm.1, s32[1,1]{1,0:T(1,128)S(6)} %copy.9.count_ref, s32[1,288]{1,0:T(1,128)} %reshape.13.order_hbm, bf16[288,384]{1,0:T(8,128)(2,1)} %bitcast.9, ...), custom_call_target="tpu_custom_call" | custom-call | tf_op jit(solution)/shard_map/prepare/pallas_call | solution.py:102
  39.9 319.0 %exchange.1 = (bf16[32,8,128,128]{3,2,1,0:T(8,128)(2,1)}, s32[32,8,128]{2,1,0:T(8,128)}, bf16[8,384,1536]{2,1,0:T(8,128)(2,1)}, bf16[8,384,512]{2,1,0:T(8,128)(2,1)}) custom-call(bf16[32,8,128,128]{3,2,1,0:T(8,128)(2,1)} %bitcast.7, s32[32,8,128]{2,1,0:T(8,128)} %get-tuple-element.10.code, bf16[384,1536]{1,0:T(8,128)(2,1)} %get-tuple-element.11.w), custom_call_target="tpu_custom_call" | custom-call | tf_op jit(solution)/shard_map/exchange/pallas_call | solution.py:252
  358.8 18.6 %half.1 = bf16[4,288,384]{2,1,0:T(8,128)(2,1)} custom-call(s32[32,8,128]{2,1,0:T(8,128)} %get-tuple-element.12.code_hbm, bf16[256,128,128]{2,1,0:T(8,128)(2,1)} %bitcast.8, bf16[8,384,1536]{2,1,0:T(8,128)(2,1)} %get-tuple-element.14.w_hbm, bf16[8,384,512]{2,1,0:T(8,128)(2,1)} %get-tuple-element.15.theirs_hbm), custom_call_target="tpu_custom_call" | custom-call | tf_op jit(solution)/shard_map/half/pallas_call | solution.py:334
  377.5 68.7 %finish.1 = bf16[9,384,128]{2,1,0:T(8,128)(2,1)} custom-call(bf16[4,288,384]{2,1,0:T(8,128)(2,1)} %half.1, bf16[8,384,1536]{2,1,0:T(8,128)(2,1)} %get-tuple-element.14.w_hbm), custom_call_target="tpu_custom_call" | custom-call | tf_op jit(solution)/shard_map/finish/pallas_call | solution.py:549
  446.2 1.5 slice_bitcast_fusion.1
  447.8 2.1 slice_bitcast_fusion

commit v3 on v2

--- a/solution.py
+++ b/solution.py
@@ -18,7 +18,8 @@
 K_HALF = NO // 2
 CHUNK = 32
 PARTS = 8
-Q = 8
+Q = 12
+W_SHAPE = (Q, SPAN // 4, 512)
 VMEM = pltpu.VMEM
 LIMIT = 60 * 2**20
 ANY = pl.BlockSpec(memory_space=pl.ANY)
@@ -28,7 +29,7 @@
 
 def prepare_kernel(vec_hbm, pair_hbm, count_ref, order_hbm, occ_hbm, vir_hbm, blocks_ref,
                    send_ref, code_hbm, w_hbm, vec_ref, pair_ref, order_ref, occ_ref, vir_ref,
-                   code_ref, w_ref, pos_vmem, pos_smem, sem, pos_sem, in_sems, out_sems):
+                   code_ref, w_ref, tiles, pos_vmem, pos_smem, sem, pos_sem, in_sems, out_sems):
     loads = [
         pltpu.make_async_copy(src, dst, in_sems.at[n])
         for n, (src, dst) in enumerate(
@@ -53,7 +54,7 @@
     to_smem.wait()
 
     def begin(slot, carry):
-        pltpu.make_async_copy(blocks_ref.at[slot], send_ref.at[pos_smem[0, slot]], sem).start()
+        pltpu.make_async_copy(blocks_ref.at[slot], tiles.at[pos_smem[0, slot]], sem).start()
         return carry
 
     lax.fori_loop(0, count, begin, 0)
@@ -81,19 +82,26 @@
         def _():
             for q in range(4):
                 r = 4 * half + q
-                w_ref[:, 256 * q:256 * q + 256] = vir_ref[:, NV_R * r:NV_R * r + 256]
+                head = vir_ref[:, NV_R * r:NV_R * r + 256]
                 tail = vir_ref[:, NV_R * r + 256:NV_R * r + NV_R].astype(F32)
                 occ = perm[:, NO_R * r:NO_R * r + NO_R]
                 zero = jnp.zeros((SPAN, 12), F32)
-                w_ref[:, 1024 + 128 * q:1152 + 128 * q] = jnp.concatenate([tail, occ, zero], axis=1).astype(BF16)
+                last = jnp.concatenate([tail, occ, zero], axis=1).astype(BF16)
+                for b in range(4):
+                    rows = slice(96 * b, 96 * b + 96)
+                    w_ref[4 * (q // 2) + b, :, 256 * (q % 2):256 * (q % 2) + 256] = head[rows]
+                    w_ref[8 + b, :, BLK * q:BLK * q + BLK] = last[rows]
     w_out = pltpu.make_async_copy(w_ref, w_hbm, out_sems.at[1])
     w_out.start()
 
     def end(slot, carry):
-        pltpu.make_async_copy(blocks_ref.at[0], send_ref.at[0], sem).wait()
+        pltpu.make_async_copy(blocks_ref.at[0], tiles.at[0], sem).wait()
         return carry
 
     lax.fori_loop(0, count, end, 0)
+    tiles_out = pltpu.make_async_copy(tiles, send_ref, sem)
+    tiles_out.start()
+    tiles_out.wait()
     code_out.wait()
     w_out.wait()
 
@@ -104,7 +112,7 @@
         out_shape=(
             jax.ShapeDtypeStruct((N_VEC * CAP, BLK, BLK), BF16),
             jax.ShapeDtypeStruct((N_VEC, 8, BLK), I32),
-            jax.ShapeDtypeStruct((SPAN, WIDE), BF16),
+            jax.ShapeDtypeStruct(W_SHAPE, BF16),
         ),
         in_specs=[ANY, ANY, pl.BlockSpec(memory_space=pltpu.SMEM), ANY, ANY, ANY, ANY],
         out_specs=(ANY, ANY, ANY),
@@ -115,7 +123,8 @@
             VMEM((NO, SPAN), BF16),
             VMEM((SPAN, NV), BF16),
             VMEM((N_VEC, 8, BLK), I32),
-            VMEM((SPAN, WIDE), BF16),
+            VMEM(W_SHAPE, BF16),
+            VMEM((N_VEC * CAP, BLK, BLK), BF16),
             VMEM((1, SLOTS), I32),
             pltpu.SMEM((1, SLOTS), I32),
             DMA,
@@ -128,7 +137,8 @@
     )(vectors, pairs, count, order, occ, vir, blocks)
 
 
-def exchange_kernel(send, code, w, recv, rcode, wfull, theirs, lsem, tsend, trecv, csend, crecv, us, ur, ds, dr, os, orc):
+def exchange_kernel(send, code, w, recv, rcode, wfull, occ_hbm, tile_bounce, code_bounce, w_bounce, mine, theirs, occ,
+                    lsem, tsend, trecv, csend, crecv, us, ur, ds, dr, os, orc, ol):
     v, z = lax.axis_index("vec"), lax.axis_index("row")
     core, x, y = lax.rem(v, 2), lax.rem(v // 2, 4), v // 8
     up, down = lax.rem(z + 1, N_ROW), lax.rem(z + N_ROW - 1, N_ROW)
@@ -143,12 +153,10 @@
     pl.semaphore_signal(barrier, inc=1, device_id=(v, down), device_id_type=MESH)
     pl.semaphore_wait(barrier, N_VEC + 1)
 
-    own = [
-        pltpu.make_async_copy(send.at[v], recv.at[v], lsem.at[0]),
-        pltpu.make_async_copy(code.at[v], rcode.at[v], lsem.at[1]),
-        pltpu.make_async_copy(w, wfull.at[z], lsem.at[2]),
-    ]
-    for copy in own:
+    own = [(send.at[v], tile_bounce, recv.at[v]), (code.at[v], code_bounce, rcode.at[v]), (w, w_bounce, wfull.at[z])]
+    own_in = [pltpu.make_async_copy(a, b, lsem.at[n]) for n, (a, b, c) in enumerate(own)]
+    own_out = [pltpu.make_async_copy(b, c, lsem.at[n]) for n, (a, b, c) in enumerate(own)]
+    for copy in own_in:
         copy.start()
 
     def remote(src, dst, send_sem, recv_sem, device):
@@ -156,18 +164,36 @@
             src_ref=src, dst_ref=dst, send_sem=send_sem, recv_sem=recv_sem, device_id=device, device_id_type=MESH
         )
 
+    last = pl.ds(8, 4)
+
     def swap(origin, src):
-        columns = pl.ds(1024, 512)
-        return remote(src.at[:, columns], theirs.at[origin], os.at[origin], orc.at[origin], (v + 1 - 2 * core, z))
-
-    rows = SPAN // Q
+        return remote(src.at[last], theirs.at[origin], os.at[origin], orc.at[origin], (v + 1 - 2 * core, z))
+
+    def fetch(origin, src):
+        return pltpu.make_async_copy(src.at[last], mine.at[origin], ol.at[origin])
+
+    index = lax.broadcasted_iota(I32, (NO, 512), 0)
+    column = lax.broadcasted_iota(I32, (NO, 512), 1)
+    lane = column % BLK - (NV_R - 256)
+    found = (lane >= 0) & (lane < NO_R)
+    wanted = index - NO_R * (column // BLK) - lane
+    pick_mine = (found & (wanted == 4 * NO_R * core)).astype(BF16)
+    pick_theirs = (found & (wanted == 4 * NO_R * (1 - core))).astype(BF16)
+    across = (((1,), (1,)), ((), ()))
+
+    def pick_occ(origin):
+        fetch(origin, w).wait()
+        swap(origin, w).wait_recv()
+        part = lax.dot_general(
+            pick_mine, mine[origin].reshape(SPAN, 512), across, preferred_element_type=F32
+        ) + lax.dot_general(pick_theirs, theirs[origin].reshape(SPAN, 512), across, preferred_element_type=F32)
+        occ[:, pl.ds(pl.multiple_of(origin * SPAN, SPAN), SPAN)] = part.astype(BF16)
 
     def ring(step, piece, sign):
         origin = lax.rem(z - sign * step + 2 * N_ROW, N_ROW)
-        part = pl.ds(piece * rows, rows)
-        src = w.at[part] if step == 0 else wfull.at[origin, part]
+        src = w.at[piece] if step == 0 else wfull.at[origin, piece]
         ssem, rsem, to = (us, ur, up) if sign > 0 else (ds, dr, down)
-        return remote(src, wfull.at[origin, part], ssem.at[step * Q + piece], rsem.at[step * Q + piece], (v, to))
+        return remote(src, wfull.at[origin, piece], ssem.at[step * Q + piece], rsem.at[step * Q + piece], (v, to))
 
     def pieces(step, sign):
         if step < 3:
@@ -181,6 +207,7 @@
 
     lax.fori_loop(0, Q, first, 0)
     swap(z, w).start()
+    fetch(z, w).start()
 
     def target(j):
         return ((y + j // 8) % 4) * 8 + ((x + j // 2) % 4) * 2 + lax.rem(core + j, 2)
@@ -201,9 +228,17 @@
     lax.fori_loop(0, PARTS * (N_VEC - 1), give, 0)
     lax.fori_loop(1, N_VEC, give_code, 0)
 
+    for n in range(3):
+        own_in[n].wait()
+        own_out[n].start()
+
+    def origin_of(step, sign):
+        return lax.rem(z - sign * step + N_ROW, N_ROW)
+
     def pass_occ(step, sign):
-        origin = lax.rem(z - sign * step + N_ROW, N_ROW)
+        origin = origin_of(step, sign)
         swap(origin, wfull.at[origin]).start()
+        fetch(origin, wfull.at[origin]).start()
 
     for step in range(1, 4):
         for piece in range(Q):
@@ -215,6 +250,12 @@
         if step < 3:
             pass_occ(step, 1)
             pass_occ(step, -1)
+        if step == 2:
+            pick_occ(z)
+        if step == 3:
+            for sign in (1, -1):
+                pick_occ(origin_of(1, sign))
+                pick_occ(origin_of(2, sign))
 
     def finish(i, carry):
         d = lax.rem(v + i, N_VEC)
@@ -235,17 +276,22 @@
         for piece in range(low, high):
             ring(3, piece, sign).wait_recv()
     pass_occ(4, 1)
+    pick_occ(origin_of(3, 1))
+    pick_occ(origin_of(3, -1))
+    pick_occ(origin_of(4, 1))
+    occ_out = pltpu.make_async_copy(occ, occ_hbm, lsem.at[3])
+    occ_out.start()
     for sign in (1, -1):
         for step in range(4):
             low, high = pieces(step, sign)
             for piece in range(low, high):
                 ring(step, piece, sign).wait_send()
     for origin in range(N_ROW):
-        pltpu.make_async_copy(theirs.at[origin], theirs.at[origin], os.at[origin]).wait()
-        pltpu.make_async_copy(theirs.at[origin], theirs.at[origin], orc.at[origin]).wait()
+        swap(origin, w).wait_send()
     lax.fori_loop(1, N_VEC, finish, 0)
-    for copy in own:
+    for copy in own_out:
         copy.wait()
+    occ_out.wait()
 
 
 def exchange(send, code, w):
@@ -255,23 +301,32 @@
             jax.ShapeDtypeStruct(send.shape, BF16),
             jax.ShapeDtypeStruct(code.shape, I32),
             jax.ShapeDtypeStruct((N_ROW,) + w.shape, BF16),
-            jax.ShapeDtypeStruct((N_ROW, SPAN, 512), BF16),
+            jax.ShapeDtypeStruct((NO, NAO), BF16),
         ),
         in_specs=[ANY] * 3,
         out_specs=(ANY,) * 4,
-        scratch_shapes=[DMA((3,))] + [DMA((N_VEC,))] * 4 + [DMA((4 * Q,))] * 4 + [DMA((N_ROW,))] * 2,
+        scratch_shapes=[
+            VMEM((CAP, BLK, BLK), BF16),
+            VMEM((8, BLK), I32),
+            VMEM(W_SHAPE, BF16),
+            VMEM((N_ROW, 4) + W_SHAPE[1:], BF16),
+            VMEM((N_ROW, 4) + W_SHAPE[1:], BF16),
+            VMEM((NO, NAO), BF16),
+            DMA((4,)),
+        ]
+        + [DMA((N_VEC,))] * 4
+        + [DMA((4 * Q,))] * 4
+        + [DMA((N_ROW,))] * 3,
         compiler_params=pltpu.CompilerParams(collective_id=0, has_side_effects=True, vmem_limit_bytes=LIMIT),
         name="exchange",
     )(send, code, w)
 
 
-def half_kernel(code_hbm, tiles_ref, w_hbm, theirs_hbm, out_ref, tiles, dense, occ, own, theirs, code_ref, sems, more):
+def half_kernel(code_hbm, tiles_ref, occ_hbm, out_ref, tiles, dense, occ, code_ref, sems, more):
     group = 32
-    core = lax.rem(lax.axis_index("vec"), 2)
     others = [
         pltpu.make_async_copy(code_hbm, code_ref, more.at[0]),
-        pltpu.make_async_copy(w_hbm.at[:, :, pl.ds(1024, 512)], own, more.at[1]),
-        pltpu.make_async_copy(theirs_hbm, theirs, more.at[2]),
+        pltpu.make_async_copy(occ_hbm, occ, more.at[1]),
     ]
     for load in others:
         load.start()
@@ -291,19 +346,6 @@
     lax.fori_loop(0, VEC_DEV * TALL, clear, 0)
     for load in others:
         load.wait()
-    index = lax.broadcasted_iota(I32, (NO, 512), 0)
-    column = lax.broadcasted_iota(I32, (NO, 512), 1)
-    lane = column % BLK - (NV_R - 256)
-    found = (lane >= 0) & (lane < NO_R)
-    wanted = index - NO_R * (column // BLK) - lane
-    pick_own = (found & (wanted == 4 * NO_R * core)).astype(BF16)
-    pick_theirs = (found & (wanted == 4 * NO_R * (1 - core))).astype(BF16)
-    across = (((1,), (1,)), ((), ()))
-    for r in range(N_ROW):
-        occ[:, SPAN * r:SPAN * r + SPAN] = (
-            lax.dot_general(pick_own, own[r], across, preferred_element_type=F32)
-            + lax.dot_general(pick_theirs, theirs[r], across, preferred_element_type=F32)
-        ).astype(BF16)
 
     def place(n, carry):
         code = code_ref[n // CAP, 0, lax.rem(n, CAP)] - 1
@@ -330,28 +372,26 @@
             out_ref[j, :, BLK * block:BLK * block + BLK] = product[:, BLK * n:BLK * n + BLK]
 
 
-def half_transform(code, tiles, w, theirs):
+def half_transform(code, tiles, occ):
     return pl.pallas_call(
         half_kernel,
         out_shape=jax.ShapeDtypeStruct((VEC_DEV, NO, SPAN), BF16),
-        in_specs=[ANY] * 4,
+        in_specs=[ANY] * 3,
         out_specs=IN_VMEM,
         scratch_shapes=[
             VMEM((SLOTS, BLK, BLK), BF16),
             VMEM((VEC_DEV * TALL, BLK, NAO), F32),
             VMEM((NO, NAO), BF16),
-            VMEM((N_ROW, SPAN, 512), BF16),
-            VMEM((N_ROW, SPAN, 512), BF16),
             pltpu.SMEM((N_VEC, 8, BLK), I32),
             DMA((SLOTS // 32,)),
-            DMA((3,)),
+            DMA((2,)),
         ],
         compiler_params=pltpu.CompilerParams(vmem_limit_bytes=LIMIT),
         name="half",
-    )(code, tiles, w, theirs)
-
-
-def finish_kernel(half, w_hbm, out_ref, w, held, total, chunk, taken, wide, wsem, lsem, hsend, hrecv, ssend, srecv, csend, crecv, x_sem, y_sem):
+    )(code, tiles, occ)
+
+
+def finish_kernel(half, w_hbm, out_ref, w, held, total, picks, chunk, taken, wide, wsem, lsem, hsend, hrecv, ssend, srecv, csend, crecv, x_sem, y_sem):
     v, z = lax.axis_index("vec"), lax.axis_index("row")
     chip, core = v // 2, lax.rem(v, 2)
     giver = z // 4
@@ -449,64 +489,80 @@
     for i in range(1, 4):
         pl.semaphore_signal(y_sem, inc=1, device_id=along_y(i), device_id_type=MESH)
 
+    row = lax.broadcasted_iota(I32, (N_VEC * CHUNK, NO), 0)
+    source = lax.broadcasted_iota(I32, (N_VEC * CHUNK, NO), 1)
+    inside = row % CHUNK
+    base = row // CHUNK * NO_V
+    for t in range(3):
+        picks[t] = ((inside // NO_V == t) & (base + inside % NO_V == source)).astype(BF16)
+
+    place = chip * N_ROW + z
+
+    def start_final(u):
+        def body(i, carry):
+            n = lax.rem(i * 37 + v * 2, 2 * N_VEC)
+            to, q = n // 2, 2 * u + lax.rem(n, 2)
+            src = chunk.at[q, pl.ds(pl.multiple_of(to * CHUNK, CHUNK), CHUNK)]
+            dst = taken.at[pl.ds(pl.multiple_of(place * CHUNK, CHUNK), CHUNK)]
+            device = (to, 4 * core + q)
+            own = (to == v) & (device[1] == z)
+
+            @pl.when(jnp.logical_not(own))
+            def _():
+                remote(src, dst, csend, crecv, device).start()
+
+            @pl.when(own)
+            def _():
+                pltpu.make_async_copy(src, dst, lsem.at[1]).start()
+
+            return carry
+
+        lax.fori_loop(0, 2 * N_VEC, body, 0)
+
     sequence = (0, 1, 7, 2, 6, 3, 5, 4)
     for load in loads:
         load.wait()
+
+    def columns(g, width=512):
+        return pl.ds(pl.multiple_of(g * width, width), width)
+
     for n in range(4):
         first, second = sequence[2 * n], sequence[2 * n + 1]
         pass_on(first)
         pass_on(second)
         a, b = arrived(first), arrived(second)
         deep = jnp.concatenate([held[a], held[b]], axis=1)
-        for col in range(0, WIDE, 512):
-            part = pl.ds(col, 512)
-            block = jnp.concatenate([w[a, :, part], w[b, :, part]], axis=0)
+
+        def add(g):
+            four = pl.ds(4 * g, 4)
+            block = jnp.concatenate([w[a, four].reshape(SPAN, 512), w[b, four].reshape(SPAN, 512)], axis=0)
             product = jnp.dot(deep, block, preferred_element_type=F32)
             if n == 0:
-                total[:, part] = product
+                total[:, columns(g)] = product
             else:
-                total[:, part] += product
-
-    row = lax.broadcasted_iota(I32, (N_VEC * CHUNK, NO), 0)
-    source = lax.broadcasted_iota(I32, (N_VEC * CHUNK, NO), 1)
-    inside = row % CHUNK
-    base = row // CHUNK * NO_V
-    stacked = jnp.zeros((N_VEC * CHUNK, 4 * BLK), F32)
-    for t in range(3):
-        pick = ((inside // NO_V == t) & (base + inside % NO_V == source)).astype(BF16)
-        if t < 2:
-            columns = jnp.concatenate([total[:, 256 * q + 128 * t:256 * q + 128 * t + 128] for q in range(4)], axis=1)
-        else:
-            columns = total[:, 1024:1536]
-        stacked = stacked + jnp.dot(pick, columns.astype(BF16), preferred_element_type=F32)
-    for q in range(4):
-        chunk[q] = stacked[:, BLK * q:BLK * q + BLK].astype(BF16)
-    pl.semaphore_wait(y_sem, 3)
-
-    place = chip * N_ROW + z
-
-    def final_copy(n):
-        to, q = n // 4, lax.rem(n, 4)
-        src = chunk.at[q, pl.ds(pl.multiple_of(to * CHUNK, CHUNK), CHUNK)]
-        dst = taken.at[pl.ds(pl.multiple_of(place * CHUNK, CHUNK), CHUNK)]
-        return src, dst, (to, 4 * core + q)
-
-    def start_final(i, carry):
-        n = lax.rem(i * 37 + v * 4, 4 * N_VEC)
-        src, dst, device = final_copy(n)
-        own = (device[0] == v) & (device[1] == z)
-
-        @pl.when(jnp.logical_not(own))
-        def _():
-            remote(src, dst, csend, crecv, device).start()
-
-        @pl.when(own)
-        def _():
-            pltpu.make_async_copy(src, dst, lsem.at[1]).start()
-
-        return carry
-
-    lax.fori_loop(0, 4 * N_VEC, start_final, 0)
+                total[:, columns(g)] += product
+
+        add(2)
+        if n < 3:
+            add(0)
+            add(1)
+            continue
+        for turn in range(2):
+            u = lax.rem(z + turn, 2)
+            add(u)
+            stacked = jnp.zeros((N_VEC * CHUNK, 2 * BLK), F32)
+            for t in range(3):
+                if t < 2:
+                    taken_columns = [total[:, columns(4 * u + 2 * q + t, BLK)] for q in range(2)]
+                else:
+                    taken_columns = [total[:, columns(8 + 2 * u + q, BLK)] for q in range(2)]
+                addend = jnp.concatenate(taken_columns, axis=1).astype(BF16)
+                stacked = stacked + jnp.dot(picks[t], addend, preferred_element_type=F32)
+            for q in range(2):
+                chunk[2 * u + q] = stacked[:, BLK * q:BLK * q + BLK].astype(BF16)
+            if turn == 0:
+                pl.semaphore_wait(y_sem, 3)
+            start_final(u)
 
     def wait_half(n, carry):
         @pl.when(jnp.logical_not(to_self(n)))
@@ -552,9 +608,10 @@
         in_specs=[ANY, ANY],
         out_specs=IN_VMEM,
         scratch_shapes=[
-            VMEM((N_ROW, SPAN, WIDE), BF16),
+            VMEM((N_ROW,) + W_SHAPE, BF16),
             VMEM((N_ROW, NO, SPAN), BF16),
             VMEM((NO, WIDE), F32),
+            VMEM((3, N_VEC * CHUNK, NO), BF16),
             VMEM((4, N_VEC * CHUNK, BLK), BF16),
             VMEM((BLK * CHUNK, BLK), BF16),
             VMEM((BLK * CHUNK, BLK), F32),
@@ -580,8 +637,8 @@
     send, code, w = prepare(
         block_vector, block_pair, block_count, occ_order.reshape(1, NO), occ_coeffs.T, vir_coeffs, blocks
     )
-    tiles, codes, w_all, theirs = exchange(send.reshape(N_VEC, CAP, BLK, BLK), code, w)
-    half = half_transform(codes, tiles.reshape(SLOTS, BLK, BLK), w_all, theirs)
+    tiles, codes, w_all, occ = exchange(send.reshape(N_VEC, CAP, BLK, BLK), code, w)
+    half = half_transform(codes, tiles.reshape(SLOTS, BLK, BLK), occ)
     result = finish(half, w_all)
     return (
         result[:, :NV_R].transpose(1, 0, 2),

time: 452 us -> 203 us (0.45)
  Pallas kernels: 444 us -> 193 us
    pallas_call x1, Pallas kernels: 319 us -> 106 us  [exchange(): pl.pallas_call(exchange_kernel, out_shape=(jax.ShapeDtypeStruct(send.shap...]
    pallas_call x1, Pallas kernels: 37.3 us -> 7.1 us  [prepare(): pl.pallas_call(prepare_kernel, out_shape=(jax.ShapeDtypeStruct((N_VEC * C...]
where the time goes in v3:
time: 203 us; the launch traced here: 200 us
  Pallas kernels  193 us (95%)
  local copies, waits for them, and re-layouts  4.84 us (2%)
    pallas_call x1, Pallas kernels, exchange(): pl.pallas_call(exchange_kernel, out_shape=(jax.ShapeDtypeStruct(send.shap...  106 us
    pallas_call x1, Pallas kernels, finish(): pl.pallas_call(finish_kernel, out_shape=jax.ShapeDtypeStruct((NO_V, W_R,...  66 us
    pallas_call x1, Pallas kernels, half_transform(): pl.pallas_call(half_kernel, out_shape=jax.ShapeDtypeStruct((VEC_DEV, NO,...  14.7 us
    pallas_call x1, Pallas kernels, prepare(): pl.pallas_call(prepare_kernel, out_shape=(jax.ShapeDtypeStruct((N_VEC * C...  7.1 us

profile of v3, /device:TPU:56, one launch (start us, length us, event | category | flops | bytes accessed | tf_op | source)
XLA Modules:
  0.0 199.6 jit_solution(4609156157329135012)
XLA Ops:
  1.3 1.2 reshape.13.order_hbm
  2.5 7.1 %prepare.1 = (bf16[256,128,128]{2,1,0:T(8,128)(2,1)}, s32[32,8,128]{2,1,0:T(8,128)}, bf16[12,96,512]{2,1,0:T(8,128)(2,1)}) custom-call(s32[1,256]{1,0:T(1,128)} %vec_hbm.1, s32[1,256]{1,0:T(1,128)} %pair_hbm.1, s32[1,1]{1,0:T(1,128)S(6)} %copy.9.count_ref, s32[1,288]{1,0:T(1,128)} %reshape.13.order_hbm, bf16[288,384]{1,0:T(8,128)(2,1)} %bitcast.9, ...), custom_call_target="tpu_custom_call" | custom-call | tf_op jit(solution)/shard_map/prepare/pallas_call | solution.py:110
  9.6 105.6 %exchange.1 = (bf16[32,8,128,128]{3,2,1,0:T(8,128)(2,1)}, s32[32,8,128]{2,1,0:T(8,128)}, bf16[8,12,96,512]{3,2,1,0:T(8,128)(2,1)}, bf16[288,3072]{1,0:T(8,128)(2,1)}) custom-call(bf16[32,8,128,128]{3,2,1,0:T(8,128)(2,1)} %bitcast.7, s32[32,8,128]{2,1,0:T(8,128)} %get-tuple-element.10.code, bf16[12,96,512]{2,1,0:T(8,128)(2,1)} %get-tuple-element.11.w), custom_call_target="tpu_custom_call" | custom-call | tf_op jit(solution)/shard_map/exchange/pallas_call | solution.py:298
  115.2 14.7 %half.1 = bf16[4,288,384]{2,1,0:T(8,128)(2,1)} custom-call(s32[32,8,128]{2,1,0:T(8,128)} %get-tuple-element.12.code_hbm, bf16[256,128,128]{2,1,0:T(8,128)(2,1)} %bitcast.8, bf16[288,3072]{1,0:T(8,128)(2,1)} %get-tuple-element.14.occ_hbm), custom_call_target="tpu_custom_call" | custom-call | tf_op jit(solution)/shard_map/half/pallas_call | solution.py:376
  129.9 66.0 %finish.1 = bf16[9,384,128]{2,1,0:T(8,128)(2,1)} custom-call(bf16[4,288,384]{2,1,0:T(8,128)(2,1)} %half.1, bf16[8,12,96,512]{3,2,1,0:T(8,128)(2,1)} %get-tuple-element.15.w_hbm), custom_call_target="tpu_custom_call" | custom-call | tf_op jit(solution)/shard_map/finish/pallas_call | solution.py:605
  196.0 1.5 slice_bitcast_fusion.1
  197.5 2.1 %slice_bitcast_fusion = bf16[336,9,128]{2,0,1:T(8,128)(2,1)} fusion(bf16[9,384,128]{2,1,0:T(8,128)(2,1)} %finish.1), kind=kLoop, calls=%fused_computation | loop fusion | bytes 1548288 | tf_op jit(solution)/shard_map/transpose | solution.py:644

commit v4 on v3

--- a/solution.py
+++ b/solution.py
@@ -60,7 +60,8 @@
     lax.fori_loop(0, count, begin, 0)
 
     loads[1].wait()
-    code = vectors % VEC_DEV * PAIRS + pair_ref[...] + 1
+    pairs = pair_ref[...]
+    code = (vectors % VEC_DEV * TALL + pairs // ACROSS) * 32 + pairs % ACROSS + 1
     valid = lax.broadcasted_iota(I32, (1, SLOTS), 1) < count
     owners = lax.broadcasted_iota(I32, (N_VEC, SLOTS), 0)
     lane = lax.broadcasted_iota(I32, (N_VEC, BLK), 1)
@@ -75,7 +76,7 @@
 
     for load in loads[2:]:
         load.wait()
-    pick = (lax.broadcasted_iota(I32, (NO, NO), 0) == order_ref[...]).astype(BF16)
+    pick = (lax.broadcasted_iota(I32, (NO, NO), 0) == order_ref[...].reshape(1, NO)).astype(BF16)
     perm = lax.dot_general(occ_ref[...], pick, (((0,), (0,)), ((), ())), preferred_element_type=F32)
     for half in range(2):
         @pl.when(core == half)
@@ -119,7 +120,7 @@
         scratch_shapes=[
             VMEM((1, SLOTS), I32),
             VMEM((1, SLOTS), I32),
-            VMEM((1, NO), I32),
+            VMEM((NO,), I32),
             VMEM((NO, SPAN), BF16),
             VMEM((SPAN, NV), BF16),
             VMEM((N_VEC, 8, BLK), I32),
@@ -137,7 +138,7 @@
     )(vectors, pairs, count, order, occ, vir, blocks)
 
 
-def exchange_kernel(send, code, w, recv, rcode, wfull, occ_hbm, tile_bounce, code_bounce, w_bounce, mine, theirs, occ,
+def exchange_kernel(send, code, w, recv, code_out, wfull, occ_hbm, tile_bounce, rcode, codes, w_bounce, mine, theirs, occ,
                     lsem, tsend, trecv, csend, crecv, us, ur, ds, dr, os, orc, ol):
     v, z = lax.axis_index("vec"), lax.axis_index("row")
     core, x, y = lax.rem(v, 2), lax.rem(v // 2, 4), v // 8
@@ -153,9 +154,11 @@
     pl.semaphore_signal(barrier, inc=1, device_id=(v, down), device_id_type=MESH)
     pl.semaphore_wait(barrier, N_VEC + 1)
 
-    own = [(send.at[v], tile_bounce, recv.at[v]), (code.at[v], code_bounce, rcode.at[v]), (w, w_bounce, wfull.at[z])]
+    own = [(send.at[v], tile_bounce, recv.at[v]), (w, w_bounce, wfull.at[z])]
     own_in = [pltpu.make_async_copy(a, b, lsem.at[n]) for n, (a, b, c) in enumerate(own)]
     own_out = [pltpu.make_async_copy(b, c, lsem.at[n]) for n, (a, b, c) in enumerate(own)]
+    own_code = pltpu.make_async_copy(code.at[v], rcode.at[v], lsem.at[2])
+    own_code.start()
     for copy in own_in:
         copy.start()
 
@@ -228,7 +231,7 @@
     lax.fori_loop(0, PARTS * (N_VEC - 1), give, 0)
     lax.fori_loop(1, N_VEC, give_code, 0)
 
-    for n in range(3):
+    for n in range(2):
         own_in[n].wait()
         own_out[n].start()
 
@@ -289,9 +292,14 @@
     for origin in range(N_ROW):
         swap(origin, w).wait_send()
     lax.fori_loop(1, N_VEC, finish, 0)
+    own_code.wait()
+    codes[...] = rcode[:, 0, :]
+    codes_out = pltpu.make_async_copy(codes, code_out, lsem.at[2])
+    codes_out.start()
     for copy in own_out:
         copy.wait()
     occ_out.wait()
+    codes_out.wait()
 
 
 def exchange(send, code, w):
@@ -299,7 +307,7 @@
         exchange_kernel,
         out_shape=(
             jax.ShapeDtypeStruct(send.shape, BF16),
-            jax.ShapeDtypeStruct(code.shape, I32),
+            jax.ShapeDtypeStruct((N_VEC, BLK), I32),
             jax.ShapeDtypeStruct((N_ROW,) + w.shape, BF16),
             jax.ShapeDtypeStruct((NO, NAO), BF16),
         ),
@@ -307,7 +315,8 @@
         out_specs=(ANY,) * 4,
         scratch_shapes=[
             VMEM((CAP, BLK, BLK), BF16),
-            VMEM((8, BLK), I32),
+            VMEM((N_VEC, 8, BLK), I32),
+            VMEM((N_VEC, BLK), I32),
             VMEM(W_SHAPE, BF16),
             VMEM((N_ROW, 4) + W_SHAPE[1:], BF16),
             VMEM((N_ROW, 4) + W_SHAPE[1:], BF16),
@@ -348,19 +357,20 @@
         load.wait()
 
     def place(n, carry):
-        code = code_ref[n // CAP, 0, lax.rem(n, CAP)] - 1
-
-        @pl.when(code >= 0)
-        def _():
-            block = code // ACROSS
-            column = pl.ds(pl.multiple_of(lax.rem(code, ACROSS) * BLK, BLK), BLK)
-            dense[block, :, column] += tiles[n].astype(F32)
+        for r in range(CAP):
+            code = code_ref[n, r] - 1
+
+            @pl.when(code >= 0)
+            def _():
+                block = lax.shift_right_logical(code, 5)
+                column = pl.ds(pl.multiple_of((code & 31) * BLK, BLK), BLK)
+                dense[block, :, column] += tiles[n * CAP + r].astype(F32)
 
         return carry
 
     for n, load in enumerate(loads):
         load.wait()
-        lax.fori_loop(n * group, n * group + group, place, 0)
+        lax.fori_loop(n * group // CAP, (n + 1) * group // CAP, place, 0)
 
     for pair in range(VEC_DEV * TALL // 2):
         rows = jnp.concatenate([dense[2 * pair], dense[2 * pair + 1]], axis=0).astype(BF16)
@@ -382,7 +392,7 @@
             VMEM((SLOTS, BLK, BLK), BF16),
             VMEM((VEC_DEV * TALL, BLK, NAO), F32),
             VMEM((NO, NAO), BF16),
-            pltpu.SMEM((N_VEC, 8, BLK), I32),
+            pltpu.SMEM((N_VEC, BLK), I32),
             DMA((SLOTS // 32,)),
             DMA((2,)),
         ],
@@ -391,7 +401,7 @@
     )(code, tiles, occ)
 
 
-def finish_kernel(half, w_hbm, out_ref, w, held, total, picks, chunk, taken, wide, wsem, lsem, hsend, hrecv, ssend, srecv, csend, crecv, x_sem, y_sem):
+def finish_kernel(half, w_hbm, taken, w, held, total, picks, chunk, wsem, lsem, hsend, hrecv, ssend, srecv, csend, crecv, x_sem, y_sem):
     v, z = lax.axis_index("vec"), lax.axis_index("row")
     chip, core = v // 2, lax.rem(v, 2)
     giver = z // 4
@@ -437,60 +447,79 @@
             src_ref=src, dst_ref=dst, send_sem=send_sem, recv_sem=recv_sem, device_id=device, device_id_type=MESH
         )
 
-    def rows(h):
-        return pl.ds(pl.multiple_of(h * K_HALF, 16), K_HALF)
-
-    def send_half(n):
-        j, h = n // 2, lax.rem(n, 2)
-        return remote(half.at[j, rows(h)], held.at[z, rows(h)], hsend.at[n], hrecv.at[z], (2 * chip + h, 4 * core + j))
-
-    def to_self(n):
-        return (4 * core + n // 2 == z) & (lax.rem(n, 2) == core)
-
-    stay = pltpu.make_async_copy(half.at[lax.rem(z, 4), rows(core)], held.at[z, rows(core)], lsem.at[0])
-
-    def start_half(n, carry):
-        @pl.when(jnp.logical_not(to_self(n)))
-        def _():
-            send_half(n).start()
-
-        return carry
-
-    lax.fori_loop(0, 8, start_half, 0)
-
-    @pl.when(takes_own)
-    def _():
-        stay.start()
-
-    def swap(r):
-        return remote(held.at[r, rows(core)], held.at[r, rows(core)], ssend.at[r], srecv.at[r], (other, z))
-
-    def pass_on(i):
+    def rows(phase, h):
+        return pl.ds(K_HALF * phase + 80 * h, 80 - 16 * h)
+
+    def on_core(h, condition=True):
+        return pl.when((core == h) & condition)
+
+    def send_half(phase, j, h):
+        return remote(
+            half.at[j, rows(phase, h)], held.at[z, rows(phase, h)],
+            hsend.at[8 * phase + 2 * j + h], hrecv.at[N_ROW * phase + z], (2 * chip + h, 4 * core + j),
+        )
+
+    def not_to_self(j, h):
+        return pl.when(jnp.logical_not((4 * core + j == z) & (core == h)))
+
+    def stay(phase, h):
+        part = rows(phase, h)
+        return pltpu.make_async_copy(half.at[lax.rem(z, 4), part], held.at[z, part], lsem.at[phase])
+
+    for phase in range(2):
+        for j in range(4):
+            for h in range(2):
+                @not_to_self(j, h)
+                def _():
+                    send_half(phase, j, h).start()
+
+        for h in range(2):
+            @on_core(h, takes_own)
+            def _():
+                stay(phase, h).start()
+
+    def swap(phase, r, h):
+        part = rows(phase, h)
+        n = N_ROW * phase + r
+        return remote(held.at[r, part], held.at[r, part], ssend.at[n], srecv.at[n], (other, z))
+
+    def await_part(part, semaphore):
+        pltpu.make_async_copy(part, part, semaphore).wait()
+
+    def pass_on(phase, i):
         r = lax.rem(z + i, N_ROW)
-        if i == 0:
-            @pl.when(takes_own)
+        for h in range(2):
+            def arrived_here(phase=phase, h=h):
+                await_part(held.at[r, rows(phase, h)], hrecv.at[N_ROW * phase + r])
+
+            if i == 0:
+                @on_core(h, takes_own)
+                def _():
+                    stay(phase, h).wait()
+
+                on_core(h, jnp.logical_not(takes_own))(arrived_here)
+            else:
+                on_core(h)(arrived_here)
+
+            @on_core(h)
             def _():
-                stay.wait()
-
-            @pl.when(jnp.logical_not(takes_own))
+                swap(phase, r, h).start()
+
+    def arrived(phase, i):
+        r = lax.rem(z + i, N_ROW)
+        for h in range(2):
+            @on_core(h)
             def _():
-                pltpu.make_async_copy(held.at[r, rows(core)], held.at[r, rows(core)], hrecv.at[r]).wait()
-        else:
-            pltpu.make_async_copy(held.at[r, rows(core)], held.at[r, rows(core)], hrecv.at[r]).wait()
-        swap(r).start()
-
-    def arrived(i):
-        r = lax.rem(z + i, N_ROW)
-        theirs = held.at[r, rows(1 - core)]
-        pltpu.make_async_copy(theirs, theirs, srecv.at[r]).wait()
+                await_part(held.at[r, rows(phase, 1 - h)], srecv.at[N_ROW * phase + r])
         return r
 
     pl.semaphore_wait(x_sem, 3)
     for i in range(1, 4):
         pl.semaphore_signal(y_sem, inc=1, device_id=along_y(i), device_id_type=MESH)
 
-    row = lax.broadcasted_iota(I32, (N_VEC * CHUNK, NO), 0)
-    source = lax.broadcasted_iota(I32, (N_VEC * CHUNK, NO), 1)
+    height = N_VEC * CHUNK // 2
+    row = lax.broadcasted_iota(I32, (height, K_HALF), 0)
+    source = lax.broadcasted_iota(I32, (height, K_HALF), 1)
     inside = row % CHUNK
     base = row // CHUNK * NO_V
     for t in range(3):
@@ -498,10 +527,10 @@
 
     place = chip * N_ROW + z
 
-    def start_final(u):
+    def start_final(phase):
         def body(i, carry):
-            n = lax.rem(i * 37 + v * 2, 2 * N_VEC)
-            to, q = n // 2, 2 * u + lax.rem(n, 2)
+            n = lax.rem(i * 37 + v * 4, 2 * N_VEC)
+            to, q = n // 4 + N_VEC // 2 * phase, lax.rem(n, 4)
             src = chunk.at[q, pl.ds(pl.multiple_of(to * CHUNK, CHUNK), CHUNK)]
             dst = taken.at[pl.ds(pl.multiple_of(place * CHUNK, CHUNK), CHUNK)]
             device = (to, 4 * core + q)
@@ -513,7 +542,7 @@
 
             @pl.when(own)
             def _():
-                pltpu.make_async_copy(src, dst, lsem.at[1]).start()
+                pltpu.make_async_copy(src, dst, lsem.at[2]).start()
 
             return carry
 
@@ -522,62 +551,50 @@
     sequence = (0, 1, 7, 2, 6, 3, 5, 4)
     for load in loads:
         load.wait()
-
-    def columns(g, width=512):
-        return pl.ds(pl.multiple_of(g * width, width), width)
-
-    for n in range(4):
-        first, second = sequence[2 * n], sequence[2 * n + 1]
-        pass_on(first)
-        pass_on(second)
-        a, b = arrived(first), arrived(second)
-        deep = jnp.concatenate([held[a], held[b]], axis=1)
-
-        def add(g):
-            four = pl.ds(4 * g, 4)
-            block = jnp.concatenate([w[a, four].reshape(SPAN, 512), w[b, four].reshape(SPAN, 512)], axis=0)
-            product = jnp.dot(deep, block, preferred_element_type=F32)
-            if n == 0:
-                total[:, columns(g)] = product
+    for phase in range(2):
+        here = slice(K_HALF * phase, K_HALF * phase + K_HALF)
+        for n in range(4):
+            first, second = sequence[2 * n], sequence[2 * n + 1]
+            pass_on(phase, first)
+            pass_on(phase, second)
+            a, b = arrived(phase, first), arrived(phase, second)
+            deep = jnp.concatenate([held[a, here], held[b, here]], axis=1)
+            for g in range(3):
+                four, cols = slice(4 * g, 4 * g + 4), slice(512 * g, 512 * g + 512)
+                block = jnp.concatenate([w[a, four].reshape(SPAN, 512), w[b, four].reshape(SPAN, 512)], axis=0)
+                product = jnp.dot(deep, block, preferred_element_type=F32)
+                if n == 0:
+                    total[:, cols] = product
+                else:
+                    total[:, cols] += product
+        stacked = jnp.zeros((height, 4 * BLK), F32)
+        for t in range(3):
+            if t < 2:
+                addend = jnp.concatenate([total[:, 256 * q + BLK * t:256 * q + BLK * t + BLK] for q in range(4)], axis=1)
             else:
-                total[:, columns(g)] += product
-
-        add(2)
-        if n < 3:
-            add(0)
-            add(1)
-            continue
-        for turn in range(2):
-            u = lax.rem(z + turn, 2)
-            add(u)
-            stacked = jnp.zeros((N_VEC * CHUNK, 2 * BLK), F32)
-            for t in range(3):
-                if t < 2:
-                    taken_columns = [total[:, columns(4 * u + 2 * q + t, BLK)] for q in range(2)]
-                else:
-                    taken_columns = [total[:, columns(8 + 2 * u + q, BLK)] for q in range(2)]
-                addend = jnp.concatenate(taken_columns, axis=1).astype(BF16)
-                stacked = stacked + jnp.dot(picks[t], addend, preferred_element_type=F32)
-            for q in range(2):
-                chunk[2 * u + q] = stacked[:, BLK * q:BLK * q + BLK].astype(BF16)
-            if turn == 0:
-                pl.semaphore_wait(y_sem, 3)
-            start_final(u)
-
-    def wait_half(n, carry):
-        @pl.when(jnp.logical_not(to_self(n)))
-        def _():
-            send_half(n).wait_send()
-
-        return carry
-
-    lax.fori_loop(0, 8, wait_half, 0)
-
-    def wait_swap(r, carry):
-        swap(r).wait_send()
-        return carry
-
-    lax.fori_loop(0, N_ROW, wait_swap, 0)
+                addend = total[:, 1024:1536]
+            stacked = stacked + jnp.dot(picks[t], addend.astype(BF16), preferred_element_type=F32)
+        for q in range(4):
+            chunk[q, height * phase:height * phase + height] = stacked[:, BLK * q:BLK * q + BLK].astype(BF16)
+        if phase == 0:
+            pl.semaphore_wait(y_sem, 3)
+        start_final(phase)
+
+    for phase in range(2):
+        for j in range(4):
+            for h in range(2):
+                @not_to_self(j, h)
+                def _():
+                    send_half(phase, j, h).wait_send()
+
+        for h in range(2):
+            @on_core(h)
+            def _():
+                def wait_swap(r, carry):
+                    swap(phase, r, h).wait_send()
+                    return carry
+
+                lax.fori_loop(0, N_ROW, wait_swap, 0)
 
     def wait_chunks(count):
         part = taken.at[pl.ds(0, count * CHUNK)]
@@ -588,39 +605,31 @@
     def _():
         wait_chunks(4 * N_VEC - 1)
         part = taken.at[pl.ds(0, CHUNK)]
-        pltpu.make_async_copy(part, part, lsem.at[1]).wait()
+        pltpu.make_async_copy(part, part, lsem.at[2]).wait()
 
     @pl.when(jnp.logical_not(takes_own))
     def _():
         wait_chunks(4 * N_VEC)
 
-    wide[...] = taken[...].astype(F32)
-    for t in range(3):
-        for k in range(NO_V):
-            block = wide[pl.ds(NO_V * t + k, BLK, stride=CHUNK), :]
-            out_ref[k, BLK * t:BLK * t + BLK, :] = block.T.astype(BF16)
-
 
 def finish(half, w):
     return pl.pallas_call(
         finish_kernel,
-        out_shape=jax.ShapeDtypeStruct((NO_V, W_R, BLK), BF16),
+        out_shape=jax.ShapeDtypeStruct((BLK * CHUNK, BLK), BF16),
         in_specs=[ANY, ANY],
-        out_specs=IN_VMEM,
+        out_specs=ANY,
         scratch_shapes=[
             VMEM((N_ROW,) + W_SHAPE, BF16),
             VMEM((N_ROW, NO, SPAN), BF16),
-            VMEM((NO, WIDE), F32),
-            VMEM((3, N_VEC * CHUNK, NO), BF16),
+            VMEM((K_HALF, WIDE), F32),
+            VMEM((3, N_VEC * CHUNK // 2, K_HALF), BF16),
             VMEM((4, N_VEC * CHUNK, BLK), BF16),
-            VMEM((BLK * CHUNK, BLK), BF16),
-            VMEM((BLK * CHUNK, BLK), F32),
             DMA((N_ROW,)),
-            DMA((2,)),
-            DMA((8,)),
-            DMA((N_ROW,)),
-            DMA((N_ROW,)),
-            DMA((N_ROW,)),
+            DMA((3,)),
+            DMA((2 * 8,)),
+            DMA((2 * N_ROW,)),
+            DMA((2 * N_ROW,)),
+            DMA((2 * N_ROW,)),
             DMA,
             DMA,
             pltpu.SemaphoreType.REGULAR,
@@ -633,17 +642,41 @@
     )(half, w)
 
 
+def arrange_kernel(taken, ov_ref, oo_ref, wide):
+    wide[...] = taken[...].astype(F32)
+    for t in range(3):
+        for k in range(NO_V):
+            block = wide[pl.ds(NO_V * t + k, BLK, stride=CHUNK), :].T.astype(BF16)
+            if t < 2:
+                ov_ref[k, BLK * t:BLK * t + BLK, :] = block
+            else:
+                ov_ref[k, 256:NV_R, :] = block[:NV_R - 256]
+                oo_ref[k] = block[NV_R - 256:W_R - 256 - 12]
+
+
+def arrange(taken):
+    return pl.pallas_call(
+        arrange_kernel,
+        out_shape=(
+            jax.ShapeDtypeStruct((NO_V, NV_R, BLK), BF16),
+            jax.ShapeDtypeStruct((NO_V, NO_R, BLK), BF16),
+        ),
+        in_specs=[IN_VMEM],
+        out_specs=(IN_VMEM, IN_VMEM),
+        scratch_shapes=[VMEM((BLK * CHUNK, BLK), F32)],
+        compiler_params=pltpu.CompilerParams(vmem_limit_bytes=LIMIT),
+        name="arrange",
+    )(taken)
+
+
 def on_device(blocks, block_vector, block_pair, block_count, occ_order, occ_coeffs, vir_coeffs):
     send, code, w = prepare(
-        block_vector, block_pair, block_count, occ_order.reshape(1, NO), occ_coeffs.T, vir_coeffs, blocks
+        block_vector, block_pair, block_count, occ_order, occ_coeffs.T, vir_coeffs, blocks
     )
     tiles, codes, w_all, occ = exchange(send.reshape(N_VEC, CAP, BLK, BLK), code, w)
     half = half_transform(codes, tiles.reshape(SLOTS, BLK, BLK), occ)
-    result = finish(half, w_all)
-    return (
-        result[:, :NV_R].transpose(1, 0, 2),
-        result[:, NV_R:NV_R + NO_R].transpose(1, 0, 2),
-    )
+    ov, oo = arrange(finish(half, w_all))
+    return ov.transpose(1, 0, 2), oo.transpose(1, 0, 2)
 
 
 def solution(mesh):

time: 203 us -> 184 us (0.906); the launches traced: 200 us -> 184 us
  Pallas kernels: 193 us -> 182 us
  local copies, waits for them, and re-layouts: 4.84 us -> 0 us
    pallas_call x1 -> x2, Pallas kernels: 66 us -> 60.6 us  [the longest x1 57.3 us: finish(): pl.pallas_call(finish_kernel, out_shape=jax.ShapeDtypeStruct((BLK * CHUNK...]
    pallas_call x1, Pallas kernels: 14.7 us -> 10.9 us  [half_transform(): pl.pallas_call(half_kernel, out_shape=jax.ShapeDtypeStruct((VEC_DEV, NO,...]
    transpose x2 -> x0, local copies, waits for them, and re-layouts: 3.6 us -> none  [the longest x1 2.05 us: on_device(): result[:, :NV_R].transpose(1, 0, 2)]
where the time goes in v4:
time: 184 us
  Pallas kernels  182 us (99%)
    pallas_call x1, Pallas kernels, exchange(): pl.pallas_call(exchange_kernel, out_shape=(jax.ShapeDtypeStruct(send.shap...  104 us
    pallas_call x1, Pallas kernels, finish(): pl.pallas_call(finish_kernel, out_shape=jax.ShapeDtypeStruct((BLK * CHUNK...  57.3 us
    pallas_call x1, Pallas kernels, half_transform(): pl.pallas_call(half_kernel, out_shape=jax.ShapeDtypeStruct((VEC_DEV, NO,...  10.9 us
    pallas_call x1, Pallas kernels, prepare(): pl.pallas_call(prepare_kernel, out_shape=(jax.ShapeDtypeStruct((N_VEC * C...  7.38 us

profile of v4, /device:TPU:56, one launch (start us, length us, event | category | flops | bytes accessed | tf_op | source)
XLA Modules:
  0.0 183.8 jit_solution(13690431145395273274)
XLA Ops:
  1.3 7.4 %prepare.1 = (bf16[256,128,128]{2,1,0:T(8,128)(2,1)}, s32[32,8,128]{2,1,0:T(8,128)}, bf16[12,96,512]{2,1,0:T(8,128)(2,1)}) custom-call(s32[1,256]{1,0:T(1,128)} %vec_hbm.1, s32[1,256]{1,0:T(1,128)} %pair_hbm.1, s32[1,1]{1,0:T(1,128)S(6)} %copy.9.count_ref, s32[288]{0:T(512)} %order_hbm.1, bf16[288,384]{1,0:T(8,128)(2,1)} %bitcast.7, ...), custom_call_target="tpu_custom_call" | custom-call | tf_op jit(solution)/shard_map/prepare/pallas_call | solution.py:111
  8.7 103.6 %exchange.1 = (bf16[32,8,128,128]{3,2,1,0:T(8,128)(2,1)}, s32[32,128]{1,0:T(8,128)}, bf16[8,12,96,512]{3,2,1,0:T(8,128)(2,1)}, bf16[288,3072]{1,0:T(8,128)(2,1)}) custom-call(bf16[32,8,128,128]{3,2,1,0:T(8,128)(2,1)} %bitcast.5, s32[32,8,128]{2,1,0:T(8,128)} %get-tuple-element.12.code, bf16[12,96,512]{2,1,0:T(8,128)(2,1)} %get-tuple-element.13.w), custom_call_target="tpu_custom_call" | custom-call | tf_op jit(solution)/shard_map/exchange/pallas_call | solution.py:306
  112.3 10.9 %half.1 = bf16[4,288,384]{2,1,0:T(8,128)(2,1)} custom-call(s32[32,128]{1,0:T(8,128)} %get-tuple-element.14.code_hbm, bf16[256,128,128]{2,1,0:T(8,128)(2,1)} %bitcast.6, bf16[288,3072]{1,0:T(8,128)(2,1)} %get-tuple-element.16.occ_hbm), custom_call_target="tpu_custom_call" | custom-call | tf_op jit(solution)/shard_map/half/pallas_call | solution.py:386
  123.2 57.3 %finish.1.taken = bf16[4096,128]{1,0:T(8,128)(2,1)} custom-call(bf16[4,288,384]{2,1,0:T(8,128)(2,1)} %half.1, bf16[8,12,96,512]{3,2,1,0:T(8,128)(2,1)} %get-tuple-element.17.w_hbm), custom_call_target="tpu_custom_call" | custom-call | tf_op jit(solution)/shard_map/finish/pallas_call | solution.py:616
  180.5 3.3 %arrange.1 = (bf16[9,336,128]{2,1,0:T(8,128)(2,1)}, bf16[9,36,128]{2,1,0:T(8,128)(2,1)}) custom-call(bf16[4096,128]{1,0:T(8,128)(2,1)} %finish.1.taken), custom_call_target="tpu_custom_call" | custom-call | tf_op jit(solution)/shard_map/arrange/pallas_call | solution.py:658

commit v5 on v4

--- a/solution.py
+++ b/solution.py
@@ -10,6 +10,7 @@
 
 N_VEC, N_ROW, N_CHIP = 32, 8, 16
 CAP, SLOTS, BLK = 8, 256, 128
+GROUP = 32
 NAO, NO, NV, SPAN = 3072, 288, 2688, 384
 VEC_DEV, PAIRS, ACROSS, TALL = 4, 72, 24, 3
 NV_R, NO_R, NO_V = NV // N_ROW, NO // N_ROW, NO // N_VEC
@@ -48,16 +49,44 @@
     owner_col = jnp.sum(jnp.where(above == across, owner, 0), axis=1, keepdims=True)
     earlier = (owner_col == owner) & (above < across)
     rank = jnp.sum(jnp.where(earlier, 1, 0), axis=0, keepdims=True)
-    pos_vmem[...] = owner * CAP + rank
+    place = jnp.where(across[:1] < count, owner * CAP + rank, SLOTS)
+    place_col = jnp.sum(jnp.where(above == across, place, 0), axis=1, keepdims=True)
+    pos_vmem[...] = jnp.sum(jnp.where(place_col == across, above + 1, 0), axis=0, keepdims=True)
     to_smem = pltpu.make_async_copy(pos_vmem, pos_smem, pos_sem)
     to_smem.start()
     to_smem.wait()
 
-    def begin(slot, carry):
-        pltpu.make_async_copy(blocks_ref.at[slot], tiles.at[pos_smem[0, slot]], sem).start()
-        return carry
-
-    lax.fori_loop(0, count, begin, 0)
+    def load_group(group):
+        def begin(i, total):
+            target = group * GROUP + i
+            slot = pos_smem[0, target]
+
+            @pl.when(slot > 0)
+            def _():
+                pltpu.make_async_copy(blocks_ref.at[slot - 1], tiles.at[target], sem.at[group]).start()
+
+            return total + jnp.where(slot > 0, 1, 0)
+
+        return lax.fori_loop(0, GROUP, begin, 0)
+
+    def write_group(group):
+        part = pl.ds(group * GROUP, GROUP)
+        return pltpu.make_async_copy(tiles.at[part], send_ref.at[part], sem.at[group])
+
+    def pass_group(group, loaded):
+        def end(i, carry):
+            pltpu.make_async_copy(blocks_ref.at[0], tiles.at[0], sem.at[group]).wait()
+            return carry
+
+        lax.fori_loop(0, loaded, end, 0)
+        write_group(group).start()
+
+    groups = SLOTS // GROUP
+    loaded = []
+    for group in range(groups):
+        loaded.append(load_group(group))
+        if group >= 2:
+            pass_group(group - 2, loaded[group - 2])
 
     loads[1].wait()
     pairs = pair_ref[...]
@@ -90,19 +119,15 @@
                 last = jnp.concatenate([tail, occ, zero], axis=1).astype(BF16)
                 for b in range(4):
                     rows = slice(96 * b, 96 * b + 96)
-                    w_ref[4 * (q // 2) + b, :, 256 * (q % 2):256 * (q % 2) + 256] = head[rows]
-                    w_ref[8 + b, :, BLK * q:BLK * q + BLK] = last[rows]
+                    w_ref[4 + 4 * (q // 2) + b, :, 256 * (q % 2):256 * (q % 2) + 256] = head[rows]
+                    w_ref[b, :, BLK * q:BLK * q + BLK] = last[rows]
     w_out = pltpu.make_async_copy(w_ref, w_hbm, out_sems.at[1])
     w_out.start()
 
-    def end(slot, carry):
-        pltpu.make_async_copy(blocks_ref.at[0], tiles.at[0], sem).wait()
-        return carry
-
-    lax.fori_loop(0, count, end, 0)
-    tiles_out = pltpu.make_async_copy(tiles, send_ref, sem)
-    tiles_out.start()
-    tiles_out.wait()
+    for group in (groups - 2, groups - 1):
+        pass_group(group, loaded[group])
+    for group in range(groups):
+        write_group(group).wait()
     code_out.wait()
     w_out.wait()
 
@@ -128,7 +153,7 @@
             VMEM((N_VEC * CAP, BLK, BLK), BF16),
             VMEM((1, SLOTS), I32),
             pltpu.SMEM((1, SLOTS), I32),
-            DMA,
+            DMA((SLOTS // GROUP,)),
             DMA,
             DMA((5,)),
             DMA((2,)),
@@ -167,7 +192,7 @@
             src_ref=src, dst_ref=dst, send_sem=send_sem, recv_sem=recv_sem, device_id=device, device_id_type=MESH
         )
 
-    last = pl.ds(8, 4)
+    last = pl.ds(0, 4)
 
     def swap(origin, src):
         return remote(src.at[last], theirs.at[origin], os.at[origin], orc.at[origin], (v + 1 - 2 * core, z))
@@ -220,12 +245,12 @@
         j = 1 + lax.rem(n * 11, N_VEC - 1)
         d = target(j)
         spot = pl.ds(part * (CAP // PARTS), CAP // PARTS)
-        remote(send.at[d, spot], recv.at[v, spot], tsend.at[d], trecv.at[v], (d, z)).start()
+        remote(send.at[d, spot], recv.at[v, spot], tsend, trecv, (d, z)).start()
         return carry
 
     def give_code(j, carry):
         d = target(j)
-        remote(code.at[d], rcode.at[v], csend.at[d], crecv.at[v], (d, z)).start()
+        remote(code.at[d], rcode.at[v], csend, crecv, (d, z)).start()
         return carry
 
     lax.fori_loop(0, PARTS * (N_VEC - 1), give, 0)
@@ -247,43 +272,28 @@
         for piece in range(Q):
             for sign in (1, -1):
                 low, high = pieces(step, sign)
+                ring(step - 1, piece, sign).wait_recv()
                 if low <= piece < high:
-                    ring(step - 1, piece, sign).wait_recv()
                     ring(step, piece, sign).start()
-        if step < 3:
-            pass_occ(step, 1)
-            pass_occ(step, -1)
+                if piece == 3:
+                    pass_occ(step, sign)
         if step == 2:
             pick_occ(z)
-        if step == 3:
-            for sign in (1, -1):
-                pick_occ(origin_of(1, sign))
-                pick_occ(origin_of(2, sign))
-
-    def finish(i, carry):
-        d = lax.rem(v + i, N_VEC)
-        pltpu.make_async_copy(send.at[d], recv.at[d], tsend.at[d]).wait()
-        pltpu.make_async_copy(code.at[d], rcode.at[d], csend.at[d]).wait()
-        pltpu.make_async_copy(send.at[d], recv.at[d], trecv.at[d]).wait()
-        pltpu.make_async_copy(code.at[d], rcode.at[d], crecv.at[d]).wait()
-        return carry
-
-    for sign in (1, -1):
-        low, high = pieces(3, sign)
-        for piece in range(Q):
-            if not low <= piece < high:
-                ring(2, piece, sign).wait_recv()
-        pass_occ(3, sign)
-    for sign in (1, -1):
-        low, high = pieces(3, sign)
-        for piece in range(low, high):
-            ring(3, piece, sign).wait_recv()
+            pick_occ(origin_of(1, 1))
+            pick_occ(origin_of(1, -1))
+    for piece in range(4):
+        ring(3, piece, 1).wait_recv()
     pass_occ(4, 1)
-    pick_occ(origin_of(3, 1))
-    pick_occ(origin_of(3, -1))
+    for step in (2, 3):
+        for sign in (1, -1):
+            pick_occ(origin_of(step, sign))
     pick_occ(origin_of(4, 1))
     occ_out = pltpu.make_async_copy(occ, occ_hbm, lsem.at[3])
     occ_out.start()
+    for sign in (1, -1):
+        low, high = pieces(3, sign)
+        for piece in range(max(low, 4), high):
+            ring(3, piece, sign).wait_recv()
     for sign in (1, -1):
         for step in range(4):
             low, high = pieces(step, sign)
@@ -291,7 +301,9 @@
                 ring(step, piece, sign).wait_send()
     for origin in range(N_ROW):
         swap(origin, w).wait_send()
-    lax.fori_loop(1, N_VEC, finish, 0)
+    tile_part, code_part = recv.at[pl.ds(0, N_VEC - 1)], rcode.at[pl.ds(0, N_VEC - 1)]
+    for part, semaphore in ((tile_part, tsend), (code_part, csend), (tile_part, trecv), (code_part, crecv)):
+        pltpu.make_async_copy(part, part, semaphore).wait()
     own_code.wait()
     codes[...] = rcode[:, 0, :]
     codes_out = pltpu.make_async_copy(codes, code_out, lsem.at[2])
@@ -323,7 +335,7 @@
             VMEM((NO, NAO), BF16),
             DMA((4,)),
         ]
-        + [DMA((N_VEC,))] * 4
+        + [DMA] * 4
         + [DMA((4 * Q,))] * 4
         + [DMA((N_ROW,))] * 3,
         compiler_params=pltpu.CompilerParams(collective_id=0, has_side_effects=True, vmem_limit_bytes=LIMIT),
@@ -570,9 +582,9 @@
         stacked = jnp.zeros((height, 4 * BLK), F32)
         for t in range(3):
             if t < 2:
-                addend = jnp.concatenate([total[:, 256 * q + BLK * t:256 * q + BLK * t + BLK] for q in range(4)], axis=1)
+                addend = jnp.concatenate([total[:, 512 + 256 * q + BLK * t:640 + 256 * q + BLK * t] for q in range(4)], axis=1)
             else:
-                addend = total[:, 1024:1536]
+                addend = total[:, :512]
             stacked = stacked + jnp.dot(picks[t], addend.astype(BF16), preferred_element_type=F32)
         for q in range(4):
             chunk[q, height * phase:height * phase + height] = stacked[:, BLK * q:BLK * q + BLK].astype(BF16)

time: 184 us -> 185 us (level)
  no operation moved by 1% of the time
where the time goes in v5:
time: 185 us; the launch traced here: 184 us
  Pallas kernels  183 us (99%)
    pallas_call x1, Pallas kernels, exchange(): pl.pallas_call(exchange_kernel, out_shape=(jax.ShapeDtypeStruct(send.shap...  102 us
    pallas_call x1, Pallas kernels, finish(): pl.pallas_call(finish_kernel, out_shape=jax.ShapeDtypeStruct((BLK * CHUNK...  58.7 us
    pallas_call x1, Pallas kernels, half_transform(): pl.pallas_call(half_kernel, out_shape=jax.ShapeDtypeStruct((VEC_DEV, NO,...  10.7 us
    pallas_call x1, Pallas kernels, prepare(): pl.pallas_call(prepare_kernel, out_shape=(jax.ShapeDtypeStruct((N_VEC * C...  7.92 us

profile of v5, /device:TPU:56, one launch (start us, length us, event | category | flops | bytes accessed | tf_op | source)
XLA Modules:
  0.0 184.1 jit_solution(13274668119814656385)
XLA Ops:
  1.3 7.9 %prepare.1 = (bf16[256,128,128]{2,1,0:T(8,128)(2,1)}, s32[32,8,128]{2,1,0:T(8,128)}, bf16[12,96,512]{2,1,0:T(8,128)(2,1)}) custom-call(s32[1,256]{1,0:T(1,128)} %vec_hbm.1, s32[1,256]{1,0:T(1,128)} %pair_hbm.1, s32[1,1]{1,0:T(1,128)S(6)} %copy.9.count_ref, s32[288]{0:T(512)} %order_hbm.1, bf16[288,384]{1,0:T(8,128)(2,1)} %bitcast.7, ...), custom_call_target="tpu_custom_call" | custom-call | tf_op jit(solution)/shard_map/prepare/pallas_call | solution.py:136
  9.2 102.2 %exchange.1 = (bf16[32,8,128,128]{3,2,1,0:T(8,128)(2,1)}, s32[32,128]{1,0:T(8,128)}, bf16[8,12,96,512]{3,2,1,0:T(8,128)(2,1)}, bf16[288,3072]{1,0:T(8,128)(2,1)}) custom-call(bf16[32,8,128,128]{3,2,1,0:T(8,128)(2,1)} %bitcast.5, s32[32,8,128]{2,1,0:T(8,128)} %get-tuple-element.12.code, bf16[12,96,512]{2,1,0:T(8,128)(2,1)} %get-tuple-element.13.w), custom_call_target="tpu_custom_call" | custom-call | tf_op jit(solution)/shard_map/exchange/pallas_call | solution.py:318
  111.4 10.7 %half.1 = bf16[4,288,384]{2,1,0:T(8,128)(2,1)} custom-call(s32[32,128]{1,0:T(8,128)} %get-tuple-element.14.code_hbm, bf16[256,128,128]{2,1,0:T(8,128)(2,1)} %bitcast.6, bf16[288,3072]{1,0:T(8,128)(2,1)} %get-tuple-element.16.occ_hbm), custom_call_target="tpu_custom_call" | custom-call | tf_op jit(solution)/shard_map/half/pallas_call | solution.py:398
  122.1 58.7 %finish.1.taken = bf16[4096,128]{1,0:T(8,128)(2,1)} custom-call(bf16[4,288,384]{2,1,0:T(8,128)(2,1)} %half.1, bf16[8,12,96,512]{3,2,1,0:T(8,128)(2,1)} %get-tuple-element.17.w_hbm), custom_call_target="tpu_custom_call" | custom-call | tf_op jit(solution)/shard_map/finish/pallas_call | solution.py:628
  180.8 3.3 %arrange.1 = (bf16[9,336,128]{2,1,0:T(8,128)(2,1)}, bf16[9,36,128]{2,1,0:T(8,128)(2,1)}) custom-call(bf16[4096,128]{1,0:T(8,128)(2,1)} %finish.1.taken), custom_call_target="tpu_custom_call" | custom-call | tf_op jit(solution)/shard_map/arrange/pallas_call | solution.py:670

commit v6 on v5

--- a/solution.py
+++ b/solution.py
@@ -200,7 +200,9 @@
     def fetch(origin, src):
         return pltpu.make_async_copy(src.at[last], mine.at[origin], ol.at[origin])
 
-    index = lax.broadcasted_iota(I32, (NO, 512), 0)
+    line = lax.broadcasted_iota(I32, (NO, 512), 0)
+    inner = line % K_HALF
+    index = (2 * (inner // NO_V) + line // K_HALF) * NO_V + inner % NO_V
     column = lax.broadcasted_iota(I32, (NO, 512), 1)
     lane = column % BLK - (NV_R - 256)
     found = (lane >= 0) & (lane < NO_R)
@@ -479,7 +481,8 @@
         return pltpu.make_async_copy(half.at[lax.rem(z, 4), part], held.at[z, part], lsem.at[phase])
 
     for phase in range(2):
-        for j in range(4):
+        for turn in range(4):
+            j = lax.rem(z + turn, 4)
             for h in range(2):
                 @not_to_self(j, h)
                 def _():
@@ -542,8 +545,8 @@
     def start_final(phase):
         def body(i, carry):
             n = lax.rem(i * 37 + v * 4, 2 * N_VEC)
-            to, q = n // 4 + N_VEC // 2 * phase, lax.rem(n, 4)
-            src = chunk.at[q, pl.ds(pl.multiple_of(to * CHUNK, CHUNK), CHUNK)]
+            to, q = 2 * (n // 4) + phase, lax.rem(n + z, 4)
+            src = chunk.at[q, pl.ds(pl.multiple_of(height * phase + n // 4 * CHUNK, CHUNK), CHUNK)]
             dst = taken.at[pl.ds(pl.multiple_of(place * CHUNK, CHUNK), CHUNK)]
             device = (to, 4 * core + q)
             own = (to == v) & (device[1] == z)

time: 185 us -> 187 us (1.011)
  the two profiles are of different devices: /device:TPU:56 before, /device:TPU:1 now
where the time goes in v6:
time: 187 us; the launch traced here: 186 us
  Pallas kernels  185 us (99%)
    pallas_call x1, Pallas kernels, exchange(): pl.pallas_call(exchange_kernel, out_shape=(jax.ShapeDtypeStruct(send.shap...  108 us
    pallas_call x1, Pallas kernels, finish(): pl.pallas_call(finish_kernel, out_shape=jax.ShapeDtypeStruct((BLK * CHUNK...  54.6 us
    pallas_call x1, Pallas kernels, half_transform(): pl.pallas_call(half_kernel, out_shape=jax.ShapeDtypeStruct((VEC_DEV, NO,...  10.9 us
    pallas_call x1, Pallas kernels, prepare(): pl.pallas_call(prepare_kernel, out_shape=(jax.ShapeDtypeStruct((N_VEC * C...  8.27 us

profile of v6, /device:TPU:1, one launch (start us, length us, event | category | flops | bytes accessed | tf_op | source)
XLA Modules:
  0.0 186.2 jit_solution(14309071609852463953)
XLA Ops:
  1.3 8.3 %prepare.1 = (bf16[256,128,128]{2,1,0:T(8,128)(2,1)}, s32[32,8,128]{2,1,0:T(8,128)}, bf16[12,96,512]{2,1,0:T(8,128)(2,1)}) custom-call(s32[1,256]{1,0:T(1,128)} %vec_hbm.1, s32[1,256]{1,0:T(1,128)} %pair_hbm.1, s32[1,1]{1,0:T(1,128)S(6)} %copy.9.count_ref, s32[288]{0:T(512)} %order_hbm.1, bf16[288,384]{1,0:T(8,128)(2,1)} %bitcast.7, ...), custom_call_target="tpu_custom_call" | custom-call | tf_op jit(solution)/shard_map/prepare/pallas_call | solution.py:136
  9.6 107.9 %exchange.1 = (bf16[32,8,128,128]{3,2,1,0:T(8,128)(2,1)}, s32[32,128]{1,0:T(8,128)}, bf16[8,12,96,512]{3,2,1,0:T(8,128)(2,1)}, bf16[288,3072]{1,0:T(8,128)(2,1)}) custom-call(bf16[32,8,128,128]{3,2,1,0:T(8,128)(2,1)} %bitcast.5, s32[32,8,128]{2,1,0:T(8,128)} %get-tuple-element.12.code, bf16[12,96,512]{2,1,0:T(8,128)(2,1)} %get-tuple-element.13.w), custom_call_target="tpu_custom_call" | custom-call | tf_op jit(solution)/shard_map/exchange/pallas_call | solution.py:320
  117.4 10.9 %half.1 = bf16[4,288,384]{2,1,0:T(8,128)(2,1)} custom-call(s32[32,128]{1,0:T(8,128)} %get-tuple-element.14.code_hbm, bf16[256,128,128]{2,1,0:T(8,128)(2,1)} %bitcast.6, bf16[288,3072]{1,0:T(8,128)(2,1)} %get-tuple-element.16.occ_hbm), custom_call_target="tpu_custom_call" | custom-call | tf_op jit(solution)/shard_map/half/pallas_call | solution.py:400
  128.4 54.6 %finish.1.taken = bf16[4096,128]{1,0:T(8,128)(2,1)} custom-call(bf16[4,288,384]{2,1,0:T(8,128)(2,1)} %half.1, bf16[8,12,96,512]{3,2,1,0:T(8,128)(2,1)} %get-tuple-element.17.w_hbm), custom_call_target="tpu_custom_call" | custom-call | tf_op jit(solution)/shard_map/finish/pallas_call | solution.py:631
  183.0 3.3 %arrange.1 = (bf16[9,336,128]{2,1,0:T(8,128)(2,1)}, bf16[9,36,128]{2,1,0:T(8,128)(2,1)}) custom-call(bf16[4096,128]{1,0:T(8,128)(2,1)} %finish.1.taken), custom_call_target="tpu_custom_call" | custom-call | tf_op jit(solution)/shard_map/arrange/pallas_call | solution.py:673

commit v7 on v5

--- a/solution.py
+++ b/solution.py
@@ -10,7 +10,6 @@
 
 N_VEC, N_ROW, N_CHIP = 32, 8, 16
 CAP, SLOTS, BLK = 8, 256, 128
-GROUP = 32
 NAO, NO, NV, SPAN = 3072, 288, 2688, 384
 VEC_DEV, PAIRS, ACROSS, TALL = 4, 72, 24, 3
 NV_R, NO_R, NO_V = NV // N_ROW, NO // N_ROW, NO // N_VEC
@@ -18,7 +17,6 @@
 WIDE = 4 * W_R
 K_HALF = NO // 2
 CHUNK = 32
-PARTS = 8
 Q = 12
 W_SHAPE = (Q, SPAN // 4, 512)
 VMEM = pltpu.VMEM
@@ -28,9 +26,9 @@
 DMA = pltpu.SemaphoreType.DMA
 
 
-def prepare_kernel(vec_hbm, pair_hbm, count_ref, order_hbm, occ_hbm, vir_hbm, blocks_ref,
-                   send_ref, code_hbm, w_hbm, vec_ref, pair_ref, order_ref, occ_ref, vir_ref,
-                   code_ref, w_ref, tiles, pos_vmem, pos_smem, sem, pos_sem, in_sems, out_sems):
+def prepare_kernel(vec_hbm, pair_hbm, count_ref, order_hbm, occ_hbm, vir_hbm,
+                   source_hbm, code_hbm, w_hbm, vec_ref, pair_ref, order_ref, occ_ref, vir_ref,
+                   code_ref, w_ref, source_ref, in_sems, out_sems):
     loads = [
         pltpu.make_async_copy(src, dst, in_sems.at[n])
         for n, (src, dst) in enumerate(
@@ -51,42 +49,10 @@
     rank = jnp.sum(jnp.where(earlier, 1, 0), axis=0, keepdims=True)
     place = jnp.where(across[:1] < count, owner * CAP + rank, SLOTS)
     place_col = jnp.sum(jnp.where(above == across, place, 0), axis=1, keepdims=True)
-    pos_vmem[...] = jnp.sum(jnp.where(place_col == across, above + 1, 0), axis=0, keepdims=True)
-    to_smem = pltpu.make_async_copy(pos_vmem, pos_smem, pos_sem)
-    to_smem.start()
-    to_smem.wait()
-
-    def load_group(group):
-        def begin(i, total):
-            target = group * GROUP + i
-            slot = pos_smem[0, target]
-
-            @pl.when(slot > 0)
-            def _():
-                pltpu.make_async_copy(blocks_ref.at[slot - 1], tiles.at[target], sem.at[group]).start()
-
-            return total + jnp.where(slot > 0, 1, 0)
-
-        return lax.fori_loop(0, GROUP, begin, 0)
-
-    def write_group(group):
-        part = pl.ds(group * GROUP, GROUP)
-        return pltpu.make_async_copy(tiles.at[part], send_ref.at[part], sem.at[group])
-
-    def pass_group(group, loaded):
-        def end(i, carry):
-            pltpu.make_async_copy(blocks_ref.at[0], tiles.at[0], sem.at[group]).wait()
-            return carry
-
-        lax.fori_loop(0, loaded, end, 0)
-        write_group(group).start()
-
-    groups = SLOTS // GROUP
-    loaded = []
-    for group in range(groups):
-        loaded.append(load_group(group))
-        if group >= 2:
-            pass_group(group - 2, loaded[group - 2])
+    source = jnp.sum(jnp.where(place_col == across, above, 0), axis=0, keepdims=True)
+    source_ref[...] = jnp.broadcast_to(source, (8, SLOTS))
+    source_out = pltpu.make_async_copy(source_ref, source_hbm, out_sems.at[2])
+    source_out.start()
 
     loads[1].wait()
     pairs = pair_ref[...]
@@ -124,23 +90,20 @@
     w_out = pltpu.make_async_copy(w_ref, w_hbm, out_sems.at[1])
     w_out.start()
 
-    for group in (groups - 2, groups - 1):
-        pass_group(group, loaded[group])
-    for group in range(groups):
-        write_group(group).wait()
+    source_out.wait()
     code_out.wait()
     w_out.wait()
 
 
-def prepare(vectors, pairs, count, order, occ, vir, blocks):
+def prepare(vectors, pairs, count, order, occ, vir):
     return pl.pallas_call(
         prepare_kernel,
         out_shape=(
-            jax.ShapeDtypeStruct((N_VEC * CAP, BLK, BLK), BF16),
+            jax.ShapeDtypeStruct((8, SLOTS), I32),
             jax.ShapeDtypeStruct((N_VEC, 8, BLK), I32),
             jax.ShapeDtypeStruct(W_SHAPE, BF16),
         ),
-        in_specs=[ANY, ANY, pl.BlockSpec(memory_space=pltpu.SMEM), ANY, ANY, ANY, ANY],
+        in_specs=[ANY, ANY, pl.BlockSpec(memory_space=pltpu.SMEM), ANY, ANY, ANY],
         out_specs=(ANY, ANY, ANY),
         scratch_shapes=[
             VMEM((1, SLOTS), I32),
@@ -150,24 +113,24 @@
             VMEM((SPAN, NV), BF16),
             VMEM((N_VEC, 8, BLK), I32),
             VMEM(W_SHAPE, BF16),
-            VMEM((N_VEC * CAP, BLK, BLK), BF16),
-            VMEM((1, SLOTS), I32),
-            pltpu.SMEM((1, SLOTS), I32),
-            DMA((SLOTS // GROUP,)),
-            DMA,
+            VMEM((8, SLOTS), I32),
             DMA((5,)),
-            DMA((2,)),
+            DMA((3,)),
         ],
         compiler_params=pltpu.CompilerParams(vmem_limit_bytes=LIMIT),
         name="prepare",
-    )(vectors, pairs, count, order, occ, vir, blocks)
-
-
-def exchange_kernel(send, code, w, recv, code_out, wfull, occ_hbm, tile_bounce, rcode, codes, w_bounce, mine, theirs, occ,
+    )(vectors, pairs, count, order, occ, vir)
+
+
+def exchange_kernel(blocks, source_hbm, code, w, recv, code_out, wfull, occ_hbm, tiles, send, source, rcode, codes, w_bounce, mine, theirs, occ,
                     lsem, tsend, trecv, csend, crecv, us, ur, ds, dr, os, orc, ol):
     v, z = lax.axis_index("vec"), lax.axis_index("row")
     core, x, y = lax.rem(v, 2), lax.rem(v // 2, 4), v // 8
     up, down = lax.rem(z + 1, N_ROW), lax.rem(z + N_ROW - 1, N_ROW)
+    tiles_in = pltpu.make_async_copy(blocks, tiles, lsem.at[4])
+    source_in = pltpu.make_async_copy(source_hbm, source, lsem.at[5])
+    tiles_in.start()
+    source_in.start()
     barrier = pltpu.get_barrier_semaphore()
 
     def greet(i, carry):
@@ -179,13 +142,12 @@
     pl.semaphore_signal(barrier, inc=1, device_id=(v, down), device_id_type=MESH)
     pl.semaphore_wait(barrier, N_VEC + 1)
 
-    own = [(send.at[v], tile_bounce, recv.at[v]), (w, w_bounce, wfull.at[z])]
-    own_in = [pltpu.make_async_copy(a, b, lsem.at[n]) for n, (a, b, c) in enumerate(own)]
-    own_out = [pltpu.make_async_copy(b, c, lsem.at[n]) for n, (a, b, c) in enumerate(own)]
+    own_w_in = pltpu.make_async_copy(w, w_bounce, lsem.at[1])
+    own_w_out = pltpu.make_async_copy(w_bounce, wfull.at[z], lsem.at[1])
+    own_tiles_out = pltpu.make_async_copy(send.at[v], recv.at[v], lsem.at[0])
     own_code = pltpu.make_async_copy(code.at[v], rcode.at[v], lsem.at[2])
     own_code.start()
-    for copy in own_in:
-        copy.start()
+    own_w_in.start()
 
     def remote(src, dst, send_sem, recv_sem, device):
         return pltpu.make_async_remote_copy(
@@ -240,12 +202,15 @@
     def target(j):
         return ((y + j // 8) % 4) * 8 + ((x + j // 2) % 4) * 2 + lax.rem(core + j, 2)
 
+    def stage(d, rank):
+        send[d, rank] = tiles[source[0, d * CAP + rank]]
+
     def give(n, carry):
         part = n // (N_VEC - 1)
         j = 1 + lax.rem(n * 11, N_VEC - 1)
         d = target(j)
-        spot = pl.ds(part * (CAP // PARTS), CAP // PARTS)
-        remote(send.at[d, spot], recv.at[v, spot], tsend, trecv, (d, z)).start()
+        stage(d, part)
+        remote(send.at[d, part], recv.at[v, part], tsend, trecv, (d, z)).start()
         return carry
 
     def give_code(j, carry):
@@ -253,12 +218,19 @@
         remote(code.at[d], rcode.at[v], csend, crecv, (d, z)).start()
         return carry
 
-    lax.fori_loop(0, PARTS * (N_VEC - 1), give, 0)
+    tiles_in.wait()
+    source_in.wait()
+    lax.fori_loop(0, CAP * (N_VEC - 1), give, 0)
     lax.fori_loop(1, N_VEC, give_code, 0)
 
-    for n in range(2):
-        own_in[n].wait()
-        own_out[n].start()
+    def stage_own(rank, carry):
+        stage(v, rank)
+        return carry
+
+    lax.fori_loop(0, CAP, stage_own, 0)
+    own_tiles_out.start()
+    own_w_in.wait()
+    own_w_out.start()
 
     def origin_of(step, sign):
         return lax.rem(z - sign * step + N_ROW, N_ROW)
@@ -308,39 +280,41 @@
     codes[...] = rcode[:, 0, :]
     codes_out = pltpu.make_async_copy(codes, code_out, lsem.at[2])
     codes_out.start()
-    for copy in own_out:
-        copy.wait()
+    own_tiles_out.wait()
+    own_w_out.wait()
     occ_out.wait()
     codes_out.wait()
 
 
-def exchange(send, code, w):
+def exchange(blocks, source, code, w):
     return pl.pallas_call(
         exchange_kernel,
         out_shape=(
-            jax.ShapeDtypeStruct(send.shape, BF16),
+            jax.ShapeDtypeStruct((N_VEC, CAP, BLK, BLK), BF16),
             jax.ShapeDtypeStruct((N_VEC, BLK), I32),
             jax.ShapeDtypeStruct((N_ROW,) + w.shape, BF16),
             jax.ShapeDtypeStruct((NO, NAO), BF16),
         ),
-        in_specs=[ANY] * 3,
+        in_specs=[ANY] * 4,
         out_specs=(ANY,) * 4,
         scratch_shapes=[
-            VMEM((CAP, BLK, BLK), BF16),
+            VMEM((SLOTS, BLK, BLK), BF16),
+            VMEM((N_VEC, CAP, BLK, BLK), BF16),
+            pltpu.SMEM((8, SLOTS), I32),
             VMEM((N_VEC, 8, BLK), I32),
             VMEM((N_VEC, BLK), I32),
             VMEM(W_SHAPE, BF16),
             VMEM((N_ROW, 4) + W_SHAPE[1:], BF16),
             VMEM((N_ROW, 4) + W_SHAPE[1:], BF16),
             VMEM((NO, NAO), BF16),
-            DMA((4,)),
+            DMA((6,)),
         ]
         + [DMA] * 4
         + [DMA((4 * Q,))] * 4
         + [DMA((N_ROW,))] * 3,
         compiler_params=pltpu.CompilerParams(collective_id=0, has_side_effects=True, vmem_limit_bytes=LIMIT),
         name="exchange",
-    )(send, code, w)
+    )(blocks, source, code, w)
 
 
 def half_kernel(code_hbm, tiles_ref, occ_hbm, out_ref, tiles, dense, occ, code_ref, sems, more):
@@ -682,10 +656,8 @@
 
 
 def on_device(blocks, block_vector, block_pair, block_count, occ_order, occ_coeffs, vir_coeffs):
-    send, code, w = prepare(
-        block_vector, block_pair, block_count, occ_order, occ_coeffs.T, vir_coeffs, blocks
-    )
-    tiles, codes, w_all, occ = exchange(send.reshape(N_VEC, CAP, BLK, BLK), code, w)
+    source, code, w = prepare(block_vector, block_pair, block_count, occ_order, occ_coeffs.T, vir_coeffs)
+    tiles, codes, w_all, occ = exchange(blocks, source, code, w)
     half = half_transform(codes, tiles.reshape(SLOTS, BLK, BLK), occ)
     ov, oo = arrange(finish(half, w_all))
     return ov.transpose(1, 0, 2), oo.transpose(1, 0, 2)

time: 185 us -> 179 us (0.968)
  Pallas kernels: 183 us -> 178 us
    pallas_call x2, Pallas kernels: 110 us -> 106 us  [the longest x1 102 us: exchange(): pl.pallas_call(exchange_kernel, out_shape=(jax.ShapeDtypeStruct((N_VEC, C...]
where the time goes in v7:
time: 179 us
  Pallas kernels  178 us (99%)
    pallas_call x1, Pallas kernels, exchange(): pl.pallas_call(exchange_kernel, out_shape=(jax.ShapeDtypeStruct((N_VEC, C...  102 us
    pallas_call x1, Pallas kernels, finish(): pl.pallas_call(finish_kernel, out_shape=jax.ShapeDtypeStruct((BLK * CHUNK...  57.2 us
    pallas_call x1, Pallas kernels, half_transform(): pl.pallas_call(half_kernel, out_shape=jax.ShapeDtypeStruct((VEC_DEV, NO,...  10.8 us
    pallas_call x1, Pallas kernels, prepare(): pl.pallas_call(prepare_kernel, out_shape=(jax.ShapeDtypeStruct((8, SLOTS)...  3.85 us

profile of v7, /device:TPU:56, one launch (start us, length us, event | category | flops | bytes accessed | tf_op | source)
XLA Modules:
  0.0 178.8 jit_solution(3352787278412102508)
XLA Ops:
  1.3 3.8 %prepare.1 = (s32[8,256]{1,0:T(8,128)}, s32[32,8,128]{2,1,0:T(8,128)}, bf16[12,96,512]{2,1,0:T(8,128)(2,1)}) custom-call(s32[1,256]{1,0:T(1,128)} %vec_hbm.1, s32[1,256]{1,0:T(1,128)} %pair_hbm.1, s32[1,1]{1,0:T(1,128)S(6)} %copy.9.count_ref, s32[288]{0:T(512)} %order_hbm.1, bf16[288,384]{1,0:T(8,128)(2,1)} %bitcast.5, bf16[384,2688]{1,0:T(8,128)(2,1)} %vir_hbm.1), custom_call_target="tpu_custom_call" | custom-call | tf_op jit(solution)/shard_map/prepare/pallas_call | solution.py:99
  5.1 102.4 %exchange.1 = (bf16[32,8,128,128]{3,2,1,0:T(8,128)(2,1)}, s32[32,128]{1,0:T(8,128)}, bf16[8,12,96,512]{3,2,1,0:T(8,128)(2,1)}, bf16[288,3072]{1,0:T(8,128)(2,1)}) custom-call(bf16[256,128,128]{2,1,0:T(8,128)(2,1)} %blocks.1, s32[8,256]{1,0:T(8,128)} %get-tuple-element.11.source_hbm, s32[32,8,128]{2,1,0:T(8,128)} %get-tuple-element.12.code, ...), custom_call_target="tpu_custom_call" | custom-call | tf_op jit(solution)/shard_map/exchange/pallas_call | solution.py:290
  107.5 10.8 %half.1 = bf16[4,288,384]{2,1,0:T(8,128)(2,1)} custom-call(s32[32,128]{1,0:T(8,128)} %get-tuple-element.14.code_hbm, bf16[256,128,128]{2,1,0:T(8,128)(2,1)} %bitcast.4, bf16[288,3072]{1,0:T(8,128)(2,1)} %get-tuple-element.16.occ_hbm), custom_call_target="tpu_custom_call" | custom-call | tf_op jit(solution)/shard_map/half/pallas_call | solution.py:372
  118.3 57.2 %finish.1.taken = bf16[4096,128]{1,0:T(8,128)(2,1)} custom-call(bf16[4,288,384]{2,1,0:T(8,128)(2,1)} %half.1, bf16[8,12,96,512]{3,2,1,0:T(8,128)(2,1)} %get-tuple-element.17.w_hbm), custom_call_target="tpu_custom_call" | custom-call | tf_op jit(solution)/shard_map/finish/pallas_call | solution.py:602
  175.6 3.3 %arrange.1 = (bf16[9,336,128]{2,1,0:T(8,128)(2,1)}, bf16[9,36,128]{2,1,0:T(8,128)(2,1)}) custom-call(bf16[4096,128]{1,0:T(8,128)(2,1)} %finish.1.taken), custom_call_target="tpu_custom_call" | custom-call | tf_op jit(solution)/shard_map/arrange/pallas_call | solution.py:644

commit v8 on v7

--- a/solution.py
+++ b/solution.py
@@ -26,18 +26,33 @@
 DMA = pltpu.SemaphoreType.DMA
 
 
-def prepare_kernel(vec_hbm, pair_hbm, count_ref, order_hbm, occ_hbm, vir_hbm,
-                   source_hbm, code_hbm, w_hbm, vec_ref, pair_ref, order_ref, occ_ref, vir_ref,
-                   code_ref, w_ref, source_ref, in_sems, out_sems):
+def exchange_kernel(vec_hbm, pair_hbm, count_ref, order_hbm, occ_part, vir_hbm, blocks, recv, code_out, wfull, occ_hbm,
+                    vec_ref, pair_ref, order_ref, occ_in, vir_ref, code_ref, w_ref, source_ref,
+                    tiles, send, source, rcode, codes, mine, theirs, occ, in_sems,
+                    lsem, tsend, trecv, csend, crecv, us, ur, ds, dr, os, orc, ol):
+    v, z = lax.axis_index("vec"), lax.axis_index("row")
+    core, x, y = lax.rem(v, 2), lax.rem(v // 2, 4), v // 8
+    up, down = lax.rem(z + 1, N_ROW), lax.rem(z + N_ROW - 1, N_ROW)
     loads = [
         pltpu.make_async_copy(src, dst, in_sems.at[n])
         for n, (src, dst) in enumerate(
-            ((vec_hbm, vec_ref), (pair_hbm, pair_ref), (order_hbm, order_ref), (occ_hbm, occ_ref), (vir_hbm, vir_ref))
+            ((vec_hbm, vec_ref), (pair_hbm, pair_ref), (order_hbm, order_ref), (occ_part, occ_in), (vir_hbm, vir_ref))
         )
     ]
     for load in loads:
         load.start()
-    core = lax.rem(lax.axis_index("vec"), 2)
+    tiles_in = pltpu.make_async_copy(blocks, tiles, lsem.at[4])
+    tiles_in.start()
+    barrier = pltpu.get_barrier_semaphore()
+
+    def greet(i, carry):
+        pl.semaphore_signal(barrier, inc=1, device_id=(lax.rem(v + i, N_VEC), z), device_id_type=MESH)
+        return carry
+
+    lax.fori_loop(1, N_VEC, greet, 0)
+    pl.semaphore_signal(barrier, inc=1, device_id=(v, up), device_id_type=MESH)
+    pl.semaphore_signal(barrier, inc=1, device_id=(v, down), device_id_type=MESH)
+
     count = count_ref[0, 0]
     loads[0].wait()
     vectors = vec_ref[...]
@@ -49,10 +64,10 @@
     rank = jnp.sum(jnp.where(earlier, 1, 0), axis=0, keepdims=True)
     place = jnp.where(across[:1] < count, owner * CAP + rank, SLOTS)
     place_col = jnp.sum(jnp.where(above == across, place, 0), axis=1, keepdims=True)
-    source = jnp.sum(jnp.where(place_col == across, above, 0), axis=0, keepdims=True)
-    source_ref[...] = jnp.broadcast_to(source, (8, SLOTS))
-    source_out = pltpu.make_async_copy(source_ref, source_hbm, out_sems.at[2])
-    source_out.start()
+    sources = jnp.sum(jnp.where(place_col == across, above, 0), axis=0, keepdims=True)
+    source_ref[...] = jnp.broadcast_to(sources, (8, SLOTS))
+    source_in = pltpu.make_async_copy(source_ref, source, lsem.at[5])
+    source_in.start()
 
     loads[1].wait()
     pairs = pair_ref[...]
@@ -60,19 +75,16 @@
     valid = lax.broadcasted_iota(I32, (1, SLOTS), 1) < count
     owners = lax.broadcasted_iota(I32, (N_VEC, SLOTS), 0)
     lane = lax.broadcasted_iota(I32, (N_VEC, BLK), 1)
-    mine = (owners == owner) & valid
+    hits = (owners == owner) & valid
     table = jnp.zeros((N_VEC, BLK), I32)
     for r in range(CAP):
-        picked = jnp.sum(jnp.where(mine & (rank == r), code, 0), axis=1, keepdims=True)
+        picked = jnp.sum(jnp.where(hits & (rank == r), code, 0), axis=1, keepdims=True)
         table = jnp.where(lane == r, picked, table)
     code_ref[...] = jnp.broadcast_to(table[:, None, :], (N_VEC, 8, BLK))
-    code_out = pltpu.make_async_copy(code_ref, code_hbm, out_sems.at[0])
-    code_out.start()
-
     for load in loads[2:]:
         load.wait()
     pick = (lax.broadcasted_iota(I32, (NO, NO), 0) == order_ref[...].reshape(1, NO)).astype(BF16)
-    perm = lax.dot_general(occ_ref[...], pick, (((0,), (0,)), ((), ())), preferred_element_type=F32)
+    perm = lax.dot_general(occ_in[...], pick, (((0,), (0,)), ((), ())), preferred_element_type=F32)
     for half in range(2):
         @pl.when(core == half)
         def _():
@@ -87,67 +99,14 @@
                     rows = slice(96 * b, 96 * b + 96)
                     w_ref[4 + 4 * (q // 2) + b, :, 256 * (q % 2):256 * (q % 2) + 256] = head[rows]
                     w_ref[b, :, BLK * q:BLK * q + BLK] = last[rows]
-    w_out = pltpu.make_async_copy(w_ref, w_hbm, out_sems.at[1])
-    w_out.start()
-
-    source_out.wait()
-    code_out.wait()
-    w_out.wait()
-
-
-def prepare(vectors, pairs, count, order, occ, vir):
-    return pl.pallas_call(
-        prepare_kernel,
-        out_shape=(
-            jax.ShapeDtypeStruct((8, SLOTS), I32),
-            jax.ShapeDtypeStruct((N_VEC, 8, BLK), I32),
-            jax.ShapeDtypeStruct(W_SHAPE, BF16),
-        ),
-        in_specs=[ANY, ANY, pl.BlockSpec(memory_space=pltpu.SMEM), ANY, ANY, ANY],
-        out_specs=(ANY, ANY, ANY),
-        scratch_shapes=[
-            VMEM((1, SLOTS), I32),
-            VMEM((1, SLOTS), I32),
-            VMEM((NO,), I32),
-            VMEM((NO, SPAN), BF16),
-            VMEM((SPAN, NV), BF16),
-            VMEM((N_VEC, 8, BLK), I32),
-            VMEM(W_SHAPE, BF16),
-            VMEM((8, SLOTS), I32),
-            DMA((5,)),
-            DMA((3,)),
-        ],
-        compiler_params=pltpu.CompilerParams(vmem_limit_bytes=LIMIT),
-        name="prepare",
-    )(vectors, pairs, count, order, occ, vir)
-
-
-def exchange_kernel(blocks, source_hbm, code, w, recv, code_out, wfull, occ_hbm, tiles, send, source, rcode, codes, w_bounce, mine, theirs, occ,
-                    lsem, tsend, trecv, csend, crecv, us, ur, ds, dr, os, orc, ol):
-    v, z = lax.axis_index("vec"), lax.axis_index("row")
-    core, x, y = lax.rem(v, 2), lax.rem(v // 2, 4), v // 8
-    up, down = lax.rem(z + 1, N_ROW), lax.rem(z + N_ROW - 1, N_ROW)
-    tiles_in = pltpu.make_async_copy(blocks, tiles, lsem.at[4])
-    source_in = pltpu.make_async_copy(source_hbm, source, lsem.at[5])
-    tiles_in.start()
-    source_in.start()
-    barrier = pltpu.get_barrier_semaphore()
-
-    def greet(i, carry):
-        pl.semaphore_signal(barrier, inc=1, device_id=(lax.rem(v + i, N_VEC), z), device_id_type=MESH)
-        return carry
-
-    lax.fori_loop(1, N_VEC, greet, 0)
-    pl.semaphore_signal(barrier, inc=1, device_id=(v, up), device_id_type=MESH)
-    pl.semaphore_signal(barrier, inc=1, device_id=(v, down), device_id_type=MESH)
+    code, w = code_ref, w_ref
     pl.semaphore_wait(barrier, N_VEC + 1)
 
-    own_w_in = pltpu.make_async_copy(w, w_bounce, lsem.at[1])
-    own_w_out = pltpu.make_async_copy(w_bounce, wfull.at[z], lsem.at[1])
+    own_w_out = pltpu.make_async_copy(w, wfull.at[z], lsem.at[1])
     own_tiles_out = pltpu.make_async_copy(send.at[v], recv.at[v], lsem.at[0])
     own_code = pltpu.make_async_copy(code.at[v], rcode.at[v], lsem.at[2])
     own_code.start()
-    own_w_in.start()
+    own_w_out.start()
 
     def remote(src, dst, send_sem, recv_sem, device):
         return pltpu.make_async_remote_copy(
@@ -229,8 +188,6 @@
 
     lax.fori_loop(0, CAP, stage_own, 0)
     own_tiles_out.start()
-    own_w_in.wait()
-    own_w_out.start()
 
     def origin_of(step, sign):
         return lax.rem(z - sign * step + N_ROW, N_ROW)
@@ -286,27 +243,35 @@
     codes_out.wait()
 
 
-def exchange(blocks, source, code, w):
+def exchange(vectors, pairs, count, order, occ, vir, blocks):
     return pl.pallas_call(
         exchange_kernel,
         out_shape=(
             jax.ShapeDtypeStruct((N_VEC, CAP, BLK, BLK), BF16),
             jax.ShapeDtypeStruct((N_VEC, BLK), I32),
-            jax.ShapeDtypeStruct((N_ROW,) + w.shape, BF16),
+            jax.ShapeDtypeStruct((N_ROW,) + W_SHAPE, BF16),
             jax.ShapeDtypeStruct((NO, NAO), BF16),
         ),
-        in_specs=[ANY] * 4,
+        in_specs=[ANY, ANY, pl.BlockSpec(memory_space=pltpu.SMEM), ANY, ANY, ANY, ANY],
         out_specs=(ANY,) * 4,
         scratch_shapes=[
+            VMEM((1, SLOTS), I32),
+            VMEM((1, SLOTS), I32),
+            VMEM((NO,), I32),
+            VMEM((NO, SPAN), BF16),
+            VMEM((SPAN, NV), BF16),
+            VMEM((N_VEC, 8, BLK), I32),
+            VMEM(W_SHAPE, BF16),
+            VMEM((8, SLOTS), I32),
             VMEM((SLOTS, BLK, BLK), BF16),
             VMEM((N_VEC, CAP, BLK, BLK), BF16),
             pltpu.SMEM((8, SLOTS), I32),
             VMEM((N_VEC, 8, BLK), I32),
             VMEM((N_VEC, BLK), I32),
-            VMEM(W_SHAPE, BF16),
             VMEM((N_ROW, 4) + W_SHAPE[1:], BF16),
             VMEM((N_ROW, 4) + W_SHAPE[1:], BF16),
             VMEM((NO, NAO), BF16),
+            DMA((5,)),
             DMA((6,)),
         ]
         + [DMA] * 4
@@ -314,7 +279,7 @@
         + [DMA((N_ROW,))] * 3,
         compiler_params=pltpu.CompilerParams(collective_id=0, has_side_effects=True, vmem_limit_bytes=LIMIT),
         name="exchange",
-    )(blocks, source, code, w)
+    )(vectors, pairs, count, order, occ, vir, blocks)
 
 
 def half_kernel(code_hbm, tiles_ref, occ_hbm, out_ref, tiles, dense, occ, code_ref, sems, more):
@@ -656,8 +621,9 @@
 
 
 def on_device(blocks, block_vector, block_pair, block_count, occ_order, occ_coeffs, vir_coeffs):
-    source, code, w = prepare(block_vector, block_pair, block_count, occ_order, occ_coeffs.T, vir_coeffs)
-    tiles, codes, w_all, occ = exchange(blocks, source, code, w)
+    tiles, codes, w_all, occ = exchange(
+        block_vector, block_pair, block_count, occ_order, occ_coeffs.T, vir_coeffs, blocks
+    )
     half = half_transform(codes, tiles.reshape(SLOTS, BLK, BLK), occ)
     ov, oo = arrange(finish(half, w_all))
     return ov.transpose(1, 0, 2), oo.transpose(1, 0, 2)

time: 179 us -> 175 us (0.978)
  Pallas kernels: 178 us -> 173 us
    pallas_call x1 -> x0, Pallas kernels: 3.85 us -> none  [prepare(): pl.pallas_call(prepare_kernel, out_shape=(jax.ShapeDtypeStruct((8, SLOTS)...]
where the time goes in v8:
time: 175 us
  Pallas kernels  173 us (99%)
    pallas_call x1, Pallas kernels, exchange(): pl.pallas_call(exchange_kernel, out_shape=(jax.ShapeDtypeStruct((N_VEC, C...  103 us
    pallas_call x1, Pallas kernels, finish(): pl.pallas_call(finish_kernel, out_shape=jax.ShapeDtypeStruct((BLK * CHUNK...  56.4 us
    pallas_call x1, Pallas kernels, half_transform(): pl.pallas_call(half_kernel, out_shape=jax.ShapeDtypeStruct((VEC_DEV, NO,...  11 us

profile of v8, /device:TPU:56, one launch (start us, length us, event | category | flops | bytes accessed | tf_op | source)
XLA Modules:
  0.0 174.7 jit_solution(5324938738691983413)
XLA Ops:
  1.3 102.7 %exchange.1 = (bf16[32,8,128,128]{3,2,1,0:T(8,128)(2,1)}, s32[32,128]{1,0:T(8,128)}, bf16[8,12,96,512]{3,2,1,0:T(8,128)(2,1)}, bf16[288,3072]{1,0:T(8,128)(2,1)}) custom-call(s32[1,256]{1,0:T(1,128)} %vec_hbm.1, s32[1,256]{1,0:T(1,128)} %pair_hbm.1, s32[1,1]{1,0:T(1,128)S(6)} %copy.9.count_ref, s32[288]{0:T(512)} %order_hbm.1, bf16[288,384]{1,0:T(8,128)(2,1)} %bitcast.5, ...), custom_call_target="tpu_custom_call" | custom-call | tf_op jit(solution)/shard_map/exchange/pallas_call | solution.py:247
  104.0 11.0 %half.1 = bf16[4,288,384]{2,1,0:T(8,128)(2,1)} custom-call(s32[32,128]{1,0:T(8,128)} %get-tuple-element.8.code_hbm, bf16[256,128,128]{2,1,0:T(8,128)(2,1)} %bitcast.4, bf16[288,3072]{1,0:T(8,128)(2,1)} %get-tuple-element.10.occ_hbm), custom_call_target="tpu_custom_call" | custom-call | tf_op jit(solution)/shard_map/half/pallas_call | solution.py:337
  115.0 56.4 %finish.1.taken = bf16[4096,128]{1,0:T(8,128)(2,1)} custom-call(bf16[4,288,384]{2,1,0:T(8,128)(2,1)} %half.1, bf16[8,12,96,512]{3,2,1,0:T(8,128)(2,1)} %get-tuple-element.11.w_hbm), custom_call_target="tpu_custom_call" | custom-call | tf_op jit(solution)/shard_map/finish/pallas_call | solution.py:567
  171.4 3.3 %arrange.1 = (bf16[9,336,128]{2,1,0:T(8,128)(2,1)}, bf16[9,36,128]{2,1,0:T(8,128)(2,1)}) custom-call(bf16[4096,128]{1,0:T(8,128)(2,1)} %finish.1.taken), custom_call_target="tpu_custom_call" | custom-call | tf_op jit(solution)/shard_map/arrange/pallas_call | solution.py:609

commit v9 on v8

--- a/solution.py
+++ b/solution.py
@@ -283,7 +283,7 @@
 
 
 def half_kernel(code_hbm, tiles_ref, occ_hbm, out_ref, tiles, dense, occ, code_ref, sems, more):
-    group = 32
+    group = 64
     others = [
         pltpu.make_async_copy(code_hbm, code_ref, more.at[0]),
         pltpu.make_async_copy(occ_hbm, occ, more.at[1]),
@@ -344,7 +344,7 @@
             VMEM((VEC_DEV * TALL, BLK, NAO), F32),
             VMEM((NO, NAO), BF16),
             pltpu.SMEM((N_VEC, BLK), I32),
-            DMA((SLOTS // 32,)),
+            DMA((SLOTS // 64,)),
             DMA((2,)),
         ],
         compiler_params=pltpu.CompilerParams(vmem_limit_bytes=LIMIT),
@@ -593,16 +593,31 @@
     )(half, w)
 
 
-def arrange_kernel(taken, ov_ref, oo_ref, wide):
-    wide[...] = taken[...].astype(F32)
-    for t in range(3):
-        for k in range(NO_V):
+def arrange_kernel(taken_hbm, ov_hbm, oo_hbm, taken, ov, oo, wide, in_sems, ov_sems, oo_sems):
+    pieces = 4
+    height = BLK * CHUNK // pieces
+    loads = []
+    for n in range(pieces):
+        part = pl.ds(n * height, height)
+        loads.append(pltpu.make_async_copy(taken_hbm.at[part], taken.at[part], in_sems.at[n]))
+        loads[n].start()
+    for n in range(pieces):
+        loads[n].wait()
+        wide[n * height:n * height + height] = taken[n * height:n * height + height].astype(F32)
+    writes = []
+    for k in range(NO_V):
+        for t in range(3):
             block = wide[pl.ds(NO_V * t + k, BLK, stride=CHUNK), :].T.astype(BF16)
             if t < 2:
-                ov_ref[k, BLK * t:BLK * t + BLK, :] = block
+                ov[k, BLK * t:BLK * t + BLK, :] = block
             else:
-                ov_ref[k, 256:NV_R, :] = block[:NV_R - 256]
-                oo_ref[k] = block[NV_R - 256:W_R - 256 - 12]
+                ov[k, 256:NV_R, :] = block[:NV_R - 256]
+                oo[k] = block[NV_R - 256:W_R - 256 - 12]
+        for source, target, sems in ((ov, ov_hbm, ov_sems), (oo, oo_hbm, oo_sems)):
+            writes.append(pltpu.make_async_copy(source.at[k], target.at[k], sems.at[k]))
+            writes[-1].start()
+    for write in writes:
+        write.wait()
 
 
 def arrange(taken):
@@ -612,9 +627,17 @@
             jax.ShapeDtypeStruct((NO_V, NV_R, BLK), BF16),
             jax.ShapeDtypeStruct((NO_V, NO_R, BLK), BF16),
         ),
-        in_specs=[IN_VMEM],
-        out_specs=(IN_VMEM, IN_VMEM),
-        scratch_shapes=[VMEM((BLK * CHUNK, BLK), F32)],
+        in_specs=[ANY],
+        out_specs=(ANY, ANY),
+        scratch_shapes=[
+            VMEM((BLK * CHUNK, BLK), BF16),
+            VMEM((NO_V, NV_R, BLK), BF16),
+            VMEM((NO_V, NO_R, BLK), BF16),
+            VMEM((BLK * CHUNK, BLK), F32),
+            DMA((4,)),
+            DMA((NO_V,)),
+            DMA((NO_V,)),
+        ],
         compiler_params=pltpu.CompilerParams(vmem_limit_bytes=LIMIT),
         name="arrange",
     )(taken)

time: 175 us -> 175 us (level)
  no operation moved by 1% of the time
where the time goes in v9:
time: 175 us
  Pallas kernels  174 us (99%)
    pallas_call x1, Pallas kernels, exchange(): pl.pallas_call(exchange_kernel, out_shape=(jax.ShapeDtypeStruct((N_VEC, C...  103 us
    pallas_call x1, Pallas kernels, finish(): pl.pallas_call(finish_kernel, out_shape=jax.ShapeDtypeStruct((BLK * CHUNK...  57.5 us
    pallas_call x1, Pallas kernels, half_transform(): pl.pallas_call(half_kernel, out_shape=jax.ShapeDtypeStruct((VEC_DEV, NO,...  10.4 us

profile of v9, /device:TPU:56, one launch (start us, length us, event | category | flops | bytes accessed | tf_op | source)
XLA Modules:
  0.0 175.0 jit_solution(17849121657505059478)
XLA Ops:
  1.3 102.7 %exchange.1 = (bf16[32,8,128,128]{3,2,1,0:T(8,128)(2,1)}, s32[32,128]{1,0:T(8,128)}, bf16[8,12,96,512]{3,2,1,0:T(8,128)(2,1)}, bf16[288,3072]{1,0:T(8,128)(2,1)}) custom-call(s32[1,256]{1,0:T(1,128)} %vec_hbm.1, s32[1,256]{1,0:T(1,128)} %pair_hbm.1, s32[1,1]{1,0:T(1,128)S(6)} %copy.9.count_ref, s32[288]{0:T(512)} %order_hbm.1, bf16[288,384]{1,0:T(8,128)(2,1)} %bitcast.5, ...), custom_call_target="tpu_custom_call" | custom-call | tf_op jit(solution)/shard_map/exchange/pallas_call | solution.py:247
  104.0 10.4 %half.1 = bf16[4,288,384]{2,1,0:T(8,128)(2,1)} custom-call(s32[32,128]{1,0:T(8,128)} %get-tuple-element.8.code_hbm, bf16[256,128,128]{2,1,0:T(8,128)(2,1)} %bitcast.4, bf16[288,3072]{1,0:T(8,128)(2,1)} %get-tuple-element.10.occ_hbm), custom_call_target="tpu_custom_call" | custom-call | tf_op jit(solution)/shard_map/half/pallas_call | solution.py:337
  114.4 57.5 %finish.1.taken_hbm = bf16[4096,128]{1,0:T(8,128)(2,1)} custom-call(bf16[4,288,384]{2,1,0:T(8,128)(2,1)} %half.1, bf16[8,12,96,512]{3,2,1,0:T(8,128)(2,1)} %get-tuple-element.11.w_hbm), custom_call_target="tpu_custom_call" | custom-call | tf_op jit(solution)/shard_map/finish/pallas_call | solution.py:567
  171.9 3.1 %arrange.1 = (bf16[9,336,128]{2,1,0:T(8,128)(2,1)}, bf16[9,36,128]{2,1,0:T(8,128)(2,1)}) custom-call(bf16[4096,128]{1,0:T(8,128)(2,1)} %finish.1.taken_hbm), custom_call_target="tpu_custom_call" | custom-call | tf_op jit(solution)/shard_map/arrange/pallas_call | solution.py:624

commit v10 on v9

--- a/solution.py
+++ b/solution.py
@@ -154,7 +154,6 @@
         ring(0, piece, -1).start()
         return carry
 
-    lax.fori_loop(0, Q, first, 0)
     swap(z, w).start()
     fetch(z, w).start()
 
@@ -179,7 +178,9 @@
 
     tiles_in.wait()
     source_in.wait()
-    lax.fori_loop(0, CAP * (N_VEC - 1), give, 0)
+    lax.fori_loop(0, N_VEC - 1, give, 0)
+    lax.fori_loop(0, Q, first, 0)
+    lax.fori_loop(N_VEC - 1, CAP * (N_VEC - 1), give, 0)
     lax.fori_loop(1, N_VEC, give_code, 0)
 
     def stage_own(rank, carry):

time: 175 us -> 175 us (level)
  no operation moved by 1% of the time
where the time goes in v10:
time: 175 us
  Pallas kernels  173 us (99%)
    pallas_call x1, Pallas kernels, exchange(): pl.pallas_call(exchange_kernel, out_shape=(jax.ShapeDtypeStruct((N_VEC, C...  103 us
    pallas_call x1, Pallas kernels, finish(): pl.pallas_call(finish_kernel, out_shape=jax.ShapeDtypeStruct((BLK * CHUNK...  57.3 us
    pallas_call x1, Pallas kernels, half_transform(): pl.pallas_call(half_kernel, out_shape=jax.ShapeDtypeStruct((VEC_DEV, NO,...  10.3 us

profile of v10, /device:TPU:56, one launch (start us, length us, event | category | flops | bytes accessed | tf_op | source)
XLA Modules:
  0.0 174.5 jit_solution(12722531570960771382)
XLA Ops:
  1.3 102.5 %exchange.1 = (bf16[32,8,128,128]{3,2,1,0:T(8,128)(2,1)}, s32[32,128]{1,0:T(8,128)}, bf16[8,12,96,512]{3,2,1,0:T(8,128)(2,1)}, bf16[288,3072]{1,0:T(8,128)(2,1)}) custom-call(s32[1,256]{1,0:T(1,128)} %vec_hbm.1, s32[1,256]{1,0:T(1,128)} %pair_hbm.1, s32[1,1]{1,0:T(1,128)S(6)} %copy.9.count_ref, s32[288]{0:T(512)} %order_hbm.1, bf16[288,384]{1,0:T(8,128)(2,1)} %bitcast.5, ...), custom_call_target="tpu_custom_call" | custom-call | tf_op jit(solution)/shard_map/exchange/pallas_call | solution.py:248
  103.8 10.3 %half.1 = bf16[4,288,384]{2,1,0:T(8,128)(2,1)} custom-call(s32[32,128]{1,0:T(8,128)} %get-tuple-element.8.code_hbm, bf16[256,128,128]{2,1,0:T(8,128)(2,1)} %bitcast.4, bf16[288,3072]{1,0:T(8,128)(2,1)} %get-tuple-element.10.occ_hbm), custom_call_target="tpu_custom_call" | custom-call | tf_op jit(solution)/shard_map/half/pallas_call | solution.py:338
  114.1 57.3 %finish.1.taken_hbm = bf16[4096,128]{1,0:T(8,128)(2,1)} custom-call(bf16[4,288,384]{2,1,0:T(8,128)(2,1)} %half.1, bf16[8,12,96,512]{3,2,1,0:T(8,128)(2,1)} %get-tuple-element.11.w_hbm), custom_call_target="tpu_custom_call" | custom-call | tf_op jit(solution)/shard_map/finish/pallas_call | solution.py:568
  171.4 3.1 %arrange.1 = (bf16[9,336,128]{2,1,0:T(8,128)(2,1)}, bf16[9,36,128]{2,1,0:T(8,128)(2,1)}) custom-call(bf16[4096,128]{1,0:T(8,128)(2,1)} %finish.1.taken_hbm), custom_call_target="tpu_custom_call" | custom-call | tf_op jit(solution)/shard_map/arrange/pallas_call | solution.py:625
